TPU v7x, 128 devices: a whole 4x4x4 slice. The times are simulated.
128 devices in a mesh: seq: 16 (over y, x), head: 8 (over z, core).
Axes of the slice: x: 4, y: 4, z: 4, core: 2. Of those that a mesh axis runs over, the one named last changes fastest.
Arguments:
- queries: bfloat16 [16384, 8192], P('seq', 'head'), may hold values from -6 to 6
- key_rows: bfloat16 [16384, 8192], P('seq', 'head'), may hold values from -6 to 6
- value_rows: bfloat16 [16384, 8192], P('seq', 'head')
- log_decay: float32 [64, 16384], P('head', 'seq')
- doc_start: int32 [16384], P('seq'), may hold values from 0 to 1, as said below
- gate_input: bfloat16 [16384, 8192], P('seq', 'head'), may hold values from -6 to 6
- norm_gain: float32 [8192], P('head'), may hold values from 0.1 to 1.9
- out_grad: bfloat16 [16384, 8192], P('seq', 'head'), may hold values from -6 to 6
Outputs:
- gated: bfloat16 [16384, 8192], P('seq', 'head')
- gate_grad: bfloat16 [16384, 8192], P('seq', 'head')
- query_grad: bfloat16 [16384, 8192], P('seq', 'head')
- key_grad: bfloat16 [16384, 8192], P('seq', 'head')
- value_grad: bfloat16 [16384, 8192], P('seq', 'head')
Inputs may be any that keep to these rules, and one draw needn't show every extreme that they name: `doc_start`: only the first 512 and the last 512 tokens of the sequence can begin a document, and each of these two ranges holds at least one start; one document runs over all devices but the first and the last.
All inputs are finite; a program needn't handle non-finite values.
Results may differ from a plain program's by a relative error of at most 0.0062.
Values sent between devices are 32-bit elements; how exact they have to be, the bound alone decides.
A program may use at most 128 MiB of HBM per device.

v0:
```python
import jax
import jax.numpy as jnp
from jax import lax
from jax.sharding import PartitionSpec as P

HEAD_TOTAL = 64
HD = 128
BLOCK = 512


epsilon = 1e-06


def passed_along(block, axis, distance):
    devices = range(lax.axis_size(axis))
    route = [(i - distance, i) for i in devices if i - distance in devices]
    return lax.ppermute(block, axis, route)


def block_terms(log_rates, start_flags):
    cumulative = jnp.cumsum(log_rates, axis=-1)
    doc_count = jnp.cumsum(start_flags, axis=-1, dtype=jnp.int32)
    length = start_flags.shape[-1]
    position = jnp.arange(length, dtype=jnp.int32)
    allowed = (doc_count[:, None] == doc_count[None, :]) & (position[:, None] >= position[None, :])
    difference = jnp.where(allowed[None], cumulative[:, :, None] - cumulative[:, None, :], 0.0)
    weight = jnp.where(allowed[None], jnp.exp(difference), 0.0)
    entering = jnp.where((doc_count == 0)[None], jnp.exp(cumulative), 0.0)
    last_doc = doc_count[-1]
    leaving = jnp.where(
        (doc_count == last_doc)[None], jnp.exp(cumulative[:, -1:] - cumulative), 0.0
    )
    passing = jnp.where(last_doc == 0, jnp.exp(cumulative[:, -1]), 0.0)
    return (weight, entering, leaving, passing)


def forward_prefix(total_pass, dev_state):

    def forward_advance(step, carried):
        received, inclusive = carried
        arrived = passed_along(inclusive, "seq", 1)
        return (arrived, total_pass[:, None, None] * arrived + dev_state)

    arrived, _ = lax.fori_loop(
        0, lax.axis_size("seq") - 1, forward_advance, (jnp.zeros_like(dev_state), dev_state)
    )
    return arrived


def backward_prefix(total_pass, dev_back):

    def backward_advance(step, carried):
        received, inclusive = carried
        arrived = passed_along(inclusive, "seq", -1)
        return (arrived, dev_back + total_pass[:, None, None] * arrived)

    arrived, _ = lax.fori_loop(
        0, lax.axis_size("seq") - 1, backward_advance, (jnp.zeros_like(dev_back), dev_back)
    )
    return arrived


def body(queries, key_rows, value_rows, log_decay, doc_start, gate_input, norm_gain, out_grad):
    row_count, width_dev = queries.shape
    head_count = width_dev // HD
    width = HEAD_TOTAL * HD
    blocks_dev = row_count // BLOCK
    query_block = queries.reshape(blocks_dev, BLOCK, head_count, HD)
    key_block = key_rows.reshape(blocks_dev, BLOCK, head_count, HD)
    value_block = value_rows.reshape(blocks_dev, BLOCK, head_count, HD)
    rate_block = log_decay.reshape(head_count, blocks_dev, BLOCK).transpose(1, 0, 2)
    start_block = doc_start.reshape(blocks_dev, BLOCK)
    weight, entering, leaving, passing = jax.vmap(block_terms)(rate_block, start_block)
    enter_rows = jnp.swapaxes(entering, 1, 2)[..., None]
    leave_rows = jnp.swapaxes(leaving, 1, 2)[..., None]
    scores = jnp.einsum(
        "nthd,nshd->nhts", query_block, key_block, preferred_element_type=jnp.float32
    )
    weights_bf = (scores * weight).astype(jnp.bfloat16)
    inside = jnp.einsum(
        "nhts,nshe->nthe", weights_bf, value_block, preferred_element_type=jnp.float32
    )
    keyed = (key_block * leave_rows).astype(jnp.bfloat16)
    local = jnp.einsum("nshd,nshe->nhde", keyed, value_block, preferred_element_type=jnp.float32)
    total_pass = jnp.ones((head_count,), jnp.float32)
    dev_state = jnp.zeros((head_count, HD, HD), jnp.float32)
    for index in range(blocks_dev):
        dev_state = passing[index][:, None, None] * dev_state + local[index]
        total_pass = total_pass * passing[index]
    incoming = forward_prefix(total_pass, dev_state)
    carried = incoming
    held_list = []
    for index in range(blocks_dev):
        held_list.append(carried.astype(jnp.bfloat16))
        carried = passing[index][:, None, None] * carried + local[index]
    held = jnp.stack(held_list)
    outside = (
        jnp.einsum("nthd,nhde->nthe", query_block, held, preferred_element_type=jnp.float32)
        * enter_rows
    )
    attn = (inside + outside).reshape(row_count, width_dev)
    sig = jax.nn.sigmoid(gate_input.astype(jnp.float32))
    grad_f = out_grad.astype(jnp.float32)
    gnorm = grad_f * sig
    squares, inner = lax.psum(
        (jnp.sum(attn * attn, axis=1), jnp.sum(gnorm * norm_gain[None, :] * attn, axis=1)), "head"
    )
    inverse = lax.rsqrt(squares / width + epsilon)
    normed = attn * inverse[:, None] * norm_gain[None, :]
    gated = (normed * sig).astype(jnp.bfloat16)
    gate_grad = (grad_f * normed * sig * (1.0 - sig)).astype(jnp.bfloat16)
    cube = inverse * inverse * inverse
    attn_grad = (
        inverse[:, None] * norm_gain[None, :] * gnorm
        - attn * cube[:, None] * inner[:, None] / width
    ).astype(jnp.bfloat16)
    agrad_block = attn_grad.reshape(blocks_dev, BLOCK, head_count, HD)
    dscore = (
        jnp.einsum("nthe,nshe->nhts", agrad_block, value_block, preferred_element_type=jnp.float32)
        * weight
    ).astype(jnp.bfloat16)
    qkeyed = (query_block * enter_rows).astype(jnp.bfloat16)
    back_local = jnp.einsum(
        "nthd,nthe->nhde", qkeyed, agrad_block, preferred_element_type=jnp.float32
    )
    dev_back = jnp.zeros((head_count, HD, HD), jnp.float32)
    for index in reversed(range(blocks_dev)):
        dev_back = back_local[index] + passing[index][:, None, None] * dev_back
    outgoing = backward_prefix(total_pass, dev_back)
    behind = outgoing
    back_list = [None] * blocks_dev
    for index in reversed(range(blocks_dev)):
        back_list[index] = behind.astype(jnp.bfloat16)
        behind = back_local[index] + passing[index][:, None, None] * behind
    back_held = jnp.stack(back_list)
    qgrad = jnp.einsum("nhts,nshd->nthd", dscore, key_block, preferred_element_type=jnp.float32)
    qgrad = qgrad + enter_rows * jnp.einsum(
        "nthe,nhde->nthd", agrad_block, held, preferred_element_type=jnp.float32
    )
    kgrad = jnp.einsum("nhts,nthd->nshd", dscore, query_block, preferred_element_type=jnp.float32)
    kgrad = kgrad + leave_rows * jnp.einsum(
        "nshe,nhde->nshd", value_block, back_held, preferred_element_type=jnp.float32
    )
    vgrad = jnp.einsum(
        "nhts,nthe->nshe", weights_bf, agrad_block, preferred_element_type=jnp.float32
    )
    vgrad = vgrad + leave_rows * jnp.einsum(
        "nshd,nhde->nshe", key_block, back_held, preferred_element_type=jnp.float32
    )
    query_grad = qgrad.reshape(row_count, width_dev).astype(jnp.bfloat16)
    key_grad = kgrad.reshape(row_count, width_dev).astype(jnp.bfloat16)
    value_grad = vgrad.reshape(row_count, width_dev).astype(jnp.bfloat16)
    return (gated, gate_grad, query_grad, key_grad, value_grad)


def solution(mesh):
    in_specs = (
        P("seq", "head"),
        P("seq", "head"),
        P("seq", "head"),
        P("head", "seq"),
        P("seq"),
        P("seq", "head"),
        P("head"),
        P("seq", "head"),
    )
    out_specs = (
        P("seq", "head"),
        P("seq", "head"),
        P("seq", "head"),
        P("seq", "head"),
        P("seq", "head"),
    )
    return jax.shard_map(body, mesh=mesh, in_specs=in_specs, out_specs=out_specs, check_vma=False)
```

profile of v0, /device:TPU:0, one launch (start us, length us, event | category | flops | bytes accessed | tf_op | source)
XLA Modules:
  0.0 629.0 jit_solution(16993417306259330545)
XLA Ops:
  24.1 239.5 %while.24 = (s32[]{:T(128)}, f32[8,128,128]{2,1,0:T(8,128)}, f32[8,128,128]{2,1,0:T(8,128)}, f32[8]{0:T(128)S(1)}, f32[8,128,128]{2,1,0:T(8,128)S(1)}, /*index=5*/s32[]{:T(128)}) while((s32[]{:T(128)}, f32[8,128,128]{2,1,0:T(8,128)}, f32[8,128,128]{2,1,0:T(8,128)}, f32[8]{0:T(128)S(1)}, f32[8,128,128]{2,1,0:T(8,128)S(1)}, ...), condition=%wide.region_5.6_spmd, body=%wide.region_4.5_spmd.sunk | while | flops 262146 | bytes 5767337 | solution.py:44
  27.6 11.4 %collective-permute-done = f32[8,128,128]{2,1,0:T(8,128)S(1)} collective-permute-done((f32[8,128,128]{2,1,0:T(8,128)}, f32[8,128,128]{2,1,0:T(8,128)S(1)}, u32[]{:S(2)}, u32[]{:S(2)}) %collective-permute-start) | collective-permute-done | bytes 524320 | tf_op jit(solution)/shard_map/while/body/eval_jaxpr/ppermute | solution.py:17
  44.3 10.6 %collective-permute-done = f32[8,128,128]{2,1,0:T(8,128)S(1)} collective-permute-done((f32[8,128,128]{2,1,0:T(8,128)}, f32[8,128,128]{2,1,0:T(8,128)S(1)}, u32[]{:S(2)}, u32[]{:S(2)}) %collective-permute-start) | collective-permute-done | bytes 524320 | tf_op jit(solution)/shard_map/while/body/eval_jaxpr/ppermute | solution.py:17
  178.6 9.7 %collective-permute-done = f32[8,128,128]{2,1,0:T(8,128)S(1)} collective-permute-done((f32[8,128,128]{2,1,0:T(8,128)}, f32[8,128,128]{2,1,0:T(8,128)S(1)}, u32[]{:S(2)}, u32[]{:S(2)}) %collective-permute-start) | collective-permute-done | bytes 524320 | tf_op jit(solution)/shard_map/while/body/eval_jaxpr/ppermute | solution.py:17
  196.5 10.7 %collective-permute-done = f32[8,128,128]{2,1,0:T(8,128)S(1)} collective-permute-done((f32[8,128,128]{2,1,0:T(8,128)}, f32[8,128,128]{2,1,0:T(8,128)S(1)}, u32[]{:S(2)}, u32[]{:S(2)}) %collective-permute-start) | collective-permute-done | bytes 524320 | tf_op jit(solution)/shard_map/while/body/eval_jaxpr/ppermute | solution.py:17
  215.5 11.9 %collective-permute-done = f32[8,128,128]{2,1,0:T(8,128)S(1)} collective-permute-done((f32[8,128,128]{2,1,0:T(8,128)}, f32[8,128,128]{2,1,0:T(8,128)S(1)}, u32[]{:S(2)}, u32[]{:S(2)}) %collective-permute-start) | collective-permute-done | bytes 524320 | tf_op jit(solution)/shard_map/while/body/eval_jaxpr/ppermute | solution.py:17
  235.9 12.0 %collective-permute-done = f32[8,128,128]{2,1,0:T(8,128)S(1)} collective-permute-done((f32[8,128,128]{2,1,0:T(8,128)}, f32[8,128,128]{2,1,0:T(8,128)S(1)}, u32[]{:S(2)}, u32[]{:S(2)}) %collective-permute-start) | collective-permute-done | bytes 524320 | tf_op jit(solution)/shard_map/while/body/eval_jaxpr/ppermute | solution.py:17
  293.4 13.5 %all-reduce = (f32[1024]{0:T(1024)S(1)}, f32[1024]{0:T(1024)S(1)}) all-reduce(f32[1024]{0:T(1024)S(1)} %bitcast.185, f32[1024]{0:T(1024)S(1)} %fusion.8), channel_id=1, replica_groups=mesh['seq'=16,'head'=8] {'head'}, use_global_device_ids=true, to_apply=%region_7.8 | all-reduce | flops 2048 | bytes 16384 | tf_op jit(solution)/shard_map/psum | solution.py:105
  332.3 252.7 %while.25 = (s32[]{:T(128)}, f32[8,128,128]{2,1,0:T(8,128)}, f32[8,128,128]{2,1,0:T(8,128)}, f32[8]{0:T(128)S(1)}, f32[8,128,128]{2,1,0:T(8,128)S(1)}, /*index=5*/s32[]{:T(128)}) while((s32[]{:T(128)}, f32[8,128,128]{2,1,0:T(8,128)}, f32[8,128,128]{2,1,0:T(8,128)}, f32[8]{0:T(128)S(1)}, f32[8,128,128]{2,1,0:T(8,128)S(1)}, ...), condition=%wide.region_11.12_spmd, body=%wide.region_10.11_spmd.sunk | while | flops 262146 | bytes 5767337 | solution.py:57
  333.6 17.2 %collective-permute-done.1 = f32[8,128,128]{2,1,0:T(8,128)S(1)} collective-permute-done((f32[8,128,128]{2,1,0:T(8,128)}, f32[8,128,128]{2,1,0:T(8,128)S(1)}, u32[]{:S(2)}, u32[]{:S(2)}) %collective-permute-start.1) | collective-permute-done | bytes 524320 | tf_op jit(solution)/shard_map/while/body/eval_jaxpr/ppermute | solution.py:17
  353.0 17.2 %collective-permute-done.1 = f32[8,128,128]{2,1,0:T(8,128)S(1)} collective-permute-done((f32[8,128,128]{2,1,0:T(8,128)}, f32[8,128,128]{2,1,0:T(8,128)S(1)}, u32[]{:S(2)}, u32[]{:S(2)}) %collective-permute-start.1) | collective-permute-done | bytes 524320 | tf_op jit(solution)/shard_map/while/body/eval_jaxpr/ppermute | solution.py:17
  372.5 16.6 %collective-permute-done.1 = f32[8,128,128]{2,1,0:T(8,128)S(1)} collective-permute-done((f32[8,128,128]{2,1,0:T(8,128)}, f32[8,128,128]{2,1,0:T(8,128)S(1)}, u32[]{:S(2)}, u32[]{:S(2)}) %collective-permute-start.1) | collective-permute-done | bytes 524320 | tf_op jit(solution)/shard_map/while/body/eval_jaxpr/ppermute | solution.py:17
  391.4 16.0 %collective-permute-done.1 = f32[8,128,128]{2,1,0:T(8,128)S(1)} collective-permute-done((f32[8,128,128]{2,1,0:T(8,128)}, f32[8,128,128]{2,1,0:T(8,128)S(1)}, u32[]{:S(2)}, u32[]{:S(2)}) %collective-permute-start.1) | collective-permute-done | bytes 524320 | tf_op jit(solution)/shard_map/while/body/eval_jaxpr/ppermute | solution.py:17
  409.6 13.7 %collective-permute-done.1 = f32[8,128,128]{2,1,0:T(8,128)S(1)} collective-permute-done((f32[8,128,128]{2,1,0:T(8,128)}, f32[8,128,128]{2,1,0:T(8,128)S(1)}, u32[]{:S(2)}, u32[]{:S(2)}) %collective-permute-start.1) | collective-permute-done | bytes 524320 | tf_op jit(solution)/shard_map/while/body/eval_jaxpr/ppermute | solution.py:17
  425.6 12.9 %collective-permute-done.1 = f32[8,128,128]{2,1,0:T(8,128)S(1)} collective-permute-done((f32[8,128,128]{2,1,0:T(8,128)}, f32[8,128,128]{2,1,0:T(8,128)S(1)}, u32[]{:S(2)}, u32[]{:S(2)}) %collective-permute-start.1) | collective-permute-done | bytes 524320 | tf_op jit(solution)/shard_map/while/body/eval_jaxpr/ppermute | solution.py:17
  440.7 11.9 %collective-permute-done.1 = f32[8,128,128]{2,1,0:T(8,128)S(1)} collective-permute-done((f32[8,128,128]{2,1,0:T(8,128)}, f32[8,128,128]{2,1,0:T(8,128)S(1)}, u32[]{:S(2)}, u32[]{:S(2)}) %collective-permute-start.1) | collective-permute-done | bytes 524320 | tf_op jit(solution)/shard_map/while/body/eval_jaxpr/ppermute | solution.py:17
  455.0 11.3 %collective-permute-done.1 = f32[8,128,128]{2,1,0:T(8,128)S(1)} collective-permute-done((f32[8,128,128]{2,1,0:T(8,128)}, f32[8,128,128]{2,1,0:T(8,128)S(1)}, u32[]{:S(2)}, u32[]{:S(2)}) %collective-permute-start.1) | collective-permute-done | bytes 524320 | tf_op jit(solution)/shard_map/while/body/eval_jaxpr/ppermute | solution.py:17
  468.5 11.5 %collective-permute-done.1 = f32[8,128,128]{2,1,0:T(8,128)S(1)} collective-permute-done((f32[8,128,128]{2,1,0:T(8,128)}, f32[8,128,128]{2,1,0:T(8,128)S(1)}, u32[]{:S(2)}, u32[]{:S(2)}) %collective-permute-start.1) | collective-permute-done | bytes 524320 | tf_op jit(solution)/shard_map/while/body/eval_jaxpr/ppermute | solution.py:17
  482.3 12.7 %collective-permute-done.1 = f32[8,128,128]{2,1,0:T(8,128)S(1)} collective-permute-done((f32[8,128,128]{2,1,0:T(8,128)}, f32[8,128,128]{2,1,0:T(8,128)S(1)}, u32[]{:S(2)}, u32[]{:S(2)}) %collective-permute-start.1) | collective-permute-done | bytes 524320 | tf_op jit(solution)/shard_map/while/body/eval_jaxpr/ppermute | solution.py:17
  497.2 14.1 %collective-permute-done.1 = f32[8,128,128]{2,1,0:T(8,128)S(1)} collective-permute-done((f32[8,128,128]{2,1,0:T(8,128)}, f32[8,128,128]{2,1,0:T(8,128)S(1)}, u32[]{:S(2)}, u32[]{:S(2)}) %collective-permute-start.1) | collective-permute-done | bytes 524320 | tf_op jit(solution)/shard_map/while/body/eval_jaxpr/ppermute | solution.py:17
  513.6 15.7 %collective-permute-done.1 = f32[8,128,128]{2,1,0:T(8,128)S(1)} collective-permute-done((f32[8,128,128]{2,1,0:T(8,128)}, f32[8,128,128]{2,1,0:T(8,128)S(1)}, u32[]{:S(2)}, u32[]{:S(2)}) %collective-permute-start.1) | collective-permute-done | bytes 524320 | tf_op jit(solution)/shard_map/while/body/eval_jaxpr/ppermute | solution.py:17
  531.6 16.8 %collective-permute-done.1 = f32[8,128,128]{2,1,0:T(8,128)S(1)} collective-permute-done((f32[8,128,128]{2,1,0:T(8,128)}, f32[8,128,128]{2,1,0:T(8,128)S(1)}, u32[]{:S(2)}, u32[]{:S(2)}) %collective-permute-start.1) | collective-permute-done | bytes 524320 | tf_op jit(solution)/shard_map/while/body/eval_jaxpr/ppermute | solution.py:17
  550.7 18.0 %collective-permute-done.1 = f32[8,128,128]{2,1,0:T(8,128)S(1)} collective-permute-done((f32[8,128,128]{2,1,0:T(8,128)}, f32[8,128,128]{2,1,0:T(8,128)S(1)}, u32[]{:S(2)}, u32[]{:S(2)}) %collective-permute-start.1) | collective-permute-done | bytes 524320 | tf_op jit(solution)/shard_map/while/body/eval_jaxpr/ppermute | solution.py:17
  571.0 13.0 %collective-permute-done.1 = f32[8,128,128]{2,1,0:T(8,128)S(1)} collective-permute-done((f32[8,128,128]{2,1,0:T(8,128)}, f32[8,128,128]{2,1,0:T(8,128)S(1)}, u32[]{:S(2)}, u32[]{:S(2)}) %collective-permute-start.1) | collective-permute-done | bytes 524320 | tf_op jit(solution)/shard_map/while/body/eval_jaxpr/ppermute | solution.py:17
  (228 shorter events, 329.4 us)
Async XLA Ops:
  24.1 15.0 %collective-permute-start = (f32[8,128,128]{2,1,0:T(8,128)}, f32[8,128,128]{2,1,0:T(8,128)S(1)}, u32[]{:S(2)}, u32[]{:S(2)}) collective-permute-start(f32[8,128,128]{2,1,0:T(8,128)} %get-tuple-element.169), channel_id=1, source_target_pairs={{0,8},{8,16},{16,24},{24,32},{32,40},{40,48},{48,56},{56,64},{64,7... | collective-permute-start | bytes 1572872 | tf_op jit(solution)/shard_map/while/body/eval_jaxpr/ppermute | solution.py:17
  40.0 14.9 %collective-permute-start = (f32[8,128,128]{2,1,0:T(8,128)}, f32[8,128,128]{2,1,0:T(8,128)S(1)}, u32[]{:S(2)}, u32[]{:S(2)}) collective-permute-start(f32[8,128,128]{2,1,0:T(8,128)} %get-tuple-element.169), channel_id=1, source_target_pairs={{0,8},{8,16},{16,24},{24,32},{32,40},{40,48},{48,56},{56,64},{64,7... | collective-permute-start | bytes 1572872 | tf_op jit(solution)/shard_map/while/body/eval_jaxpr/ppermute | solution.py:17
  55.9 14.0 %collective-permute-start = (f32[8,128,128]{2,1,0:T(8,128)}, f32[8,128,128]{2,1,0:T(8,128)S(1)}, u32[]{:S(2)}, u32[]{:S(2)}) collective-permute-start(f32[8,128,128]{2,1,0:T(8,128)} %get-tuple-element.169), channel_id=1, source_target_pairs={{0,8},{8,16},{16,24},{24,32},{32,40},{40,48},{48,56},{56,64},{64,7... | collective-permute-start | bytes 1572872 | tf_op jit(solution)/shard_map/while/body/eval_jaxpr/ppermute | solution.py:17
  111.4 13.4 %collective-permute-start = (f32[8,128,128]{2,1,0:T(8,128)}, f32[8,128,128]{2,1,0:T(8,128)S(1)}, u32[]{:S(2)}, u32[]{:S(2)}) collective-permute-start(f32[8,128,128]{2,1,0:T(8,128)} %get-tuple-element.169), channel_id=1, source_target_pairs={{0,8},{8,16},{16,24},{24,32},{32,40},{40,48},{48,56},{56,64},{64,7... | collective-permute-start | bytes 1572872 | tf_op jit(solution)/shard_map/while/body/eval_jaxpr/ppermute | solution.py:17
  125.8 13.4 %collective-permute-start = (f32[8,128,128]{2,1,0:T(8,128)}, f32[8,128,128]{2,1,0:T(8,128)S(1)}, u32[]{:S(2)}, u32[]{:S(2)}) collective-permute-start(f32[8,128,128]{2,1,0:T(8,128)} %get-tuple-element.169), channel_id=1, source_target_pairs={{0,8},{8,16},{16,24},{24,32},{32,40},{40,48},{48,56},{56,64},{64,7... | collective-permute-start | bytes 1572872 | tf_op jit(solution)/shard_map/while/body/eval_jaxpr/ppermute | solution.py:17
  140.1 14.0 %collective-permute-start = (f32[8,128,128]{2,1,0:T(8,128)}, f32[8,128,128]{2,1,0:T(8,128)S(1)}, u32[]{:S(2)}, u32[]{:S(2)}) collective-permute-start(f32[8,128,128]{2,1,0:T(8,128)} %get-tuple-element.169), channel_id=1, source_target_pairs={{0,8},{8,16},{16,24},{24,32},{32,40},{40,48},{48,56},{56,64},{64,7... | collective-permute-start | bytes 1572872 | tf_op jit(solution)/shard_map/while/body/eval_jaxpr/ppermute | solution.py:17
  155.1 15.3 %collective-permute-start = (f32[8,128,128]{2,1,0:T(8,128)}, f32[8,128,128]{2,1,0:T(8,128)S(1)}, u32[]{:S(2)}, u32[]{:S(2)}) collective-permute-start(f32[8,128,128]{2,1,0:T(8,128)} %get-tuple-element.169), channel_id=1, source_target_pairs={{0,8},{8,16},{16,24},{24,32},{32,40},{40,48},{48,56},{56,64},{64,7... | collective-permute-start | bytes 1572872 | tf_op jit(solution)/shard_map/while/body/eval_jaxpr/ppermute | solution.py:17
  171.3 17.0 %collective-permute-start = (f32[8,128,128]{2,1,0:T(8,128)}, f32[8,128,128]{2,1,0:T(8,128)S(1)}, u32[]{:S(2)}, u32[]{:S(2)}) collective-permute-start(f32[8,128,128]{2,1,0:T(8,128)} %get-tuple-element.169), channel_id=1, source_target_pairs={{0,8},{8,16},{16,24},{24,32},{32,40},{40,48},{48,56},{56,64},{64,7... | collective-permute-start | bytes 1572872 | tf_op jit(solution)/shard_map/while/body/eval_jaxpr/ppermute | solution.py:17
  189.2 18.0 %collective-permute-start = (f32[8,128,128]{2,1,0:T(8,128)}, f32[8,128,128]{2,1,0:T(8,128)S(1)}, u32[]{:S(2)}, u32[]{:S(2)}) collective-permute-start(f32[8,128,128]{2,1,0:T(8,128)} %get-tuple-element.169), channel_id=1, source_target_pairs={{0,8},{8,16},{16,24},{24,32},{32,40},{40,48},{48,56},{56,64},{64,7... | collective-permute-start | bytes 1572872 | tf_op jit(solution)/shard_map/while/body/eval_jaxpr/ppermute | solution.py:17
  208.2 19.2 %collective-permute-start = (f32[8,128,128]{2,1,0:T(8,128)}, f32[8,128,128]{2,1,0:T(8,128)S(1)}, u32[]{:S(2)}, u32[]{:S(2)}) collective-permute-start(f32[8,128,128]{2,1,0:T(8,128)} %get-tuple-element.169), channel_id=1, source_target_pairs={{0,8},{8,16},{16,24},{24,32},{32,40},{40,48},{48,56},{56,64},{64,7... | collective-permute-start | bytes 1572872 | tf_op jit(solution)/shard_map/while/body/eval_jaxpr/ppermute | solution.py:17
  228.4 19.4 %collective-permute-start = (f32[8,128,128]{2,1,0:T(8,128)}, f32[8,128,128]{2,1,0:T(8,128)S(1)}, u32[]{:S(2)}, u32[]{:S(2)}) collective-permute-start(f32[8,128,128]{2,1,0:T(8,128)} %get-tuple-element.169), channel_id=1, source_target_pairs={{0,8},{8,16},{16,24},{24,32},{32,40},{40,48},{48,56},{56,64},{64,7... | collective-permute-start | bytes 1572872 | tf_op jit(solution)/shard_map/while/body/eval_jaxpr/ppermute | solution.py:17
  248.8 13.7 %collective-permute-start = (f32[8,128,128]{2,1,0:T(8,128)}, f32[8,128,128]{2,1,0:T(8,128)S(1)}, u32[]{:S(2)}, u32[]{:S(2)}) collective-permute-start(f32[8,128,128]{2,1,0:T(8,128)} %get-tuple-element.169), channel_id=1, source_target_pairs={{0,8},{8,16},{16,24},{24,32},{32,40},{40,48},{48,56},{56,64},{64,7... | collective-permute-start | bytes 1572872 | tf_op jit(solution)/shard_map/while/body/eval_jaxpr/ppermute | solution.py:17
  332.3 18.4 %collective-permute-start.1 = (f32[8,128,128]{2,1,0:T(8,128)}, f32[8,128,128]{2,1,0:T(8,128)S(1)}, u32[]{:S(2)}, u32[]{:S(2)}) collective-permute-start(f32[8,128,128]{2,1,0:T(8,128)} %get-tuple-element.187), channel_id=1, source_target_pairs={{8,0},{16,8},{24,16},{32,24},{40,32},{48,40},{56,48},{64,56},{72,6... | collective-permute-start | bytes 1572872 | tf_op jit(solution)/shard_map/while/body/eval_jaxpr/ppermute | solution.py:17
  351.7 18.4 %collective-permute-start.1 = (f32[8,128,128]{2,1,0:T(8,128)}, f32[8,128,128]{2,1,0:T(8,128)S(1)}, u32[]{:S(2)}, u32[]{:S(2)}) collective-permute-start(f32[8,128,128]{2,1,0:T(8,128)} %get-tuple-element.187), channel_id=1, source_target_pairs={{8,0},{16,8},{24,16},{32,24},{40,32},{48,40},{56,48},{64,56},{72,6... | collective-permute-start | bytes 1572872 | tf_op jit(solution)/shard_map/while/body/eval_jaxpr/ppermute | solution.py:17
  371.2 17.9 %collective-permute-start.1 = (f32[8,128,128]{2,1,0:T(8,128)}, f32[8,128,128]{2,1,0:T(8,128)S(1)}, u32[]{:S(2)}, u32[]{:S(2)}) collective-permute-start(f32[8,128,128]{2,1,0:T(8,128)} %get-tuple-element.187), channel_id=1, source_target_pairs={{8,0},{16,8},{24,16},{32,24},{40,32},{48,40},{56,48},{64,56},{72,6... | collective-permute-start | bytes 1572872 | tf_op jit(solution)/shard_map/while/body/eval_jaxpr/ppermute | solution.py:17
  390.1 17.2 %collective-permute-start.1 = (f32[8,128,128]{2,1,0:T(8,128)}, f32[8,128,128]{2,1,0:T(8,128)S(1)}, u32[]{:S(2)}, u32[]{:S(2)}) collective-permute-start(f32[8,128,128]{2,1,0:T(8,128)} %get-tuple-element.187), channel_id=1, source_target_pairs={{8,0},{16,8},{24,16},{32,24},{40,32},{48,40},{56,48},{64,56},{72,6... | collective-permute-start | bytes 1572872 | tf_op jit(solution)/shard_map/while/body/eval_jaxpr/ppermute | solution.py:17
  408.3 15.0 %collective-permute-start.1 = (f32[8,128,128]{2,1,0:T(8,128)}, f32[8,128,128]{2,1,0:T(8,128)S(1)}, u32[]{:S(2)}, u32[]{:S(2)}) collective-permute-start(f32[8,128,128]{2,1,0:T(8,128)} %get-tuple-element.187), channel_id=1, source_target_pairs={{8,0},{16,8},{24,16},{32,24},{40,32},{48,40},{56,48},{64,56},{72,6... | collective-permute-start | bytes 1572872 | tf_op jit(solution)/shard_map/while/body/eval_jaxpr/ppermute | solution.py:17
  424.3 14.2 %collective-permute-start.1 = (f32[8,128,128]{2,1,0:T(8,128)}, f32[8,128,128]{2,1,0:T(8,128)S(1)}, u32[]{:S(2)}, u32[]{:S(2)}) collective-permute-start(f32[8,128,128]{2,1,0:T(8,128)} %get-tuple-element.187), channel_id=1, source_target_pairs={{8,0},{16,8},{24,16},{32,24},{40,32},{48,40},{56,48},{64,56},{72,6... | collective-permute-start | bytes 1572872 | tf_op jit(solution)/shard_map/while/body/eval_jaxpr/ppermute | solution.py:17
  481.0 13.9 %collective-permute-start.1 = (f32[8,128,128]{2,1,0:T(8,128)}, f32[8,128,128]{2,1,0:T(8,128)S(1)}, u32[]{:S(2)}, u32[]{:S(2)}) collective-permute-start(f32[8,128,128]{2,1,0:T(8,128)} %get-tuple-element.187), channel_id=1, source_target_pairs={{8,0},{16,8},{24,16},{32,24},{40,32},{48,40},{56,48},{64,56},{72,6... | collective-permute-start | bytes 1572872 | tf_op jit(solution)/shard_map/while/body/eval_jaxpr/ppermute | solution.py:17
  496.0 15.4 %collective-permute-start.1 = (f32[8,128,128]{2,1,0:T(8,128)}, f32[8,128,128]{2,1,0:T(8,128)S(1)}, u32[]{:S(2)}, u32[]{:S(2)}) collective-permute-start(f32[8,128,128]{2,1,0:T(8,128)} %get-tuple-element.187), channel_id=1, source_target_pairs={{8,0},{16,8},{24,16},{32,24},{40,32},{48,40},{56,48},{64,56},{72,6... | collective-permute-start | bytes 1572872 | tf_op jit(solution)/shard_map/while/body/eval_jaxpr/ppermute | solution.py:17
  512.4 17.0 %collective-permute-start.1 = (f32[8,128,128]{2,1,0:T(8,128)}, f32[8,128,128]{2,1,0:T(8,128)S(1)}, u32[]{:S(2)}, u32[]{:S(2)}) collective-permute-start(f32[8,128,128]{2,1,0:T(8,128)} %get-tuple-element.187), channel_id=1, source_target_pairs={{8,0},{16,8},{24,16},{32,24},{40,32},{48,40},{56,48},{64,56},{72,6... | collective-permute-start | bytes 1572872 | tf_op jit(solution)/shard_map/while/body/eval_jaxpr/ppermute | solution.py:17
  530.4 18.1 %collective-permute-start.1 = (f32[8,128,128]{2,1,0:T(8,128)}, f32[8,128,128]{2,1,0:T(8,128)S(1)}, u32[]{:S(2)}, u32[]{:S(2)}) collective-permute-start(f32[8,128,128]{2,1,0:T(8,128)} %get-tuple-element.187), channel_id=1, source_target_pairs={{8,0},{16,8},{24,16},{32,24},{40,32},{48,40},{56,48},{64,56},{72,6... | collective-permute-start | bytes 1572872 | tf_op jit(solution)/shard_map/while/body/eval_jaxpr/ppermute | solution.py:17
  549.4 19.3 %collective-permute-start.1 = (f32[8,128,128]{2,1,0:T(8,128)}, f32[8,128,128]{2,1,0:T(8,128)S(1)}, u32[]{:S(2)}, u32[]{:S(2)}) collective-permute-start(f32[8,128,128]{2,1,0:T(8,128)} %get-tuple-element.187), channel_id=1, source_target_pairs={{8,0},{16,8},{24,16},{32,24},{40,32},{48,40},{56,48},{64,56},{72,6... | collective-permute-start | bytes 1572872 | tf_op jit(solution)/shard_map/while/body/eval_jaxpr/ppermute | solution.py:17
  569.8 14.2 %collective-permute-start.1 = (f32[8,128,128]{2,1,0:T(8,128)}, f32[8,128,128]{2,1,0:T(8,128)S(1)}, u32[]{:S(2)}, u32[]{:S(2)}) collective-permute-start(f32[8,128,128]{2,1,0:T(8,128)} %get-tuple-element.187), channel_id=1, source_target_pairs={{8,0},{16,8},{24,16},{32,24},{40,32},{48,40},{56,48},{64,56},{72,6... | collective-permute-start | bytes 1572872 | tf_op jit(solution)/shard_map/while/body/eval_jaxpr/ppermute | solution.py:17
  (57 other events, 194.2 us)
where the time goes:
time: 639 us; the launch traced here: 629 us
  waiting for transfers between devices  355 us (56%)
  starting transfers between devices  108 us (17%)
  matrix products  57.4 us (9%)
  other arithmetic  52.7 us (8%)
  local copies, waits for them, and re-layouts  41.6 us (7%)
  blocking collectives  13.5 us (2%)
    ppermute x30, waiting for transfers between devices, passed_along(): return lax.ppermute(block, axis, route)  355 us
    ppermute x30, starting transfers between devices, passed_along(): return lax.ppermute(block, axis, route)  108 us
    unnamed x52, local copies, waits for them, and re-layouts  15.3 us
    add x15, other arithmetic, backward_advance(): return (arrived, dev_back + total_pass[:, None, None] * arrived)  14.8 us
    add x15, other arithmetic, forward_advance(): return (arrived, total_pass[:, None, None] * arrived + dev_state)  14.4 us
    psum x1, blocking collectives, body(): lax.psum((jnp.sum(attn * attn, axis=1), jnp.sum(gnorm * norm_gain[None, :...  13.5 us
  transfers between devices with their start and end apart: 30, of which 30 were waited for; matrix products, arithmetic and copies ran while one was open for 0% of the time, Pallas kernels for 0%

commit v1 on v0

v1 whole, which is shorter than its diff:
```python
import functools

import jax
import jax.numpy as jnp
from jax import lax
from jax.experimental import pallas as pl
from jax.experimental.pallas import tpu as pltpu
from jax.sharding import PartitionSpec as P

HEAD_TOTAL = 64
HD = 128
BLOCK = 512
HALF = 256
EPSILON = 1e-06
MESH = pl.DeviceIdType.MESH
F32 = jnp.float32
BF16 = jnp.bfloat16

NN = (((1,), (0,)), ((), ()))
NT = (((1,), (1,)), ((), ()))
TN = (((0,), (0,)), ((), ()))

CUM, ENTER, LEAVE, COUNT = range(4)


def mm(a, b, dims=NN):
    return lax.dot_general(a, b, dims, preferred_element_type=F32)


def pieces(x):
    hi = x.astype(BF16).astype(F32)
    rest = x - hi
    mid = rest.astype(BF16).astype(F32)
    low = (rest - mid).astype(BF16).astype(F32)
    return hi, mid, low


def running_sum(x):
    lane = lax.broadcasted_iota(jnp.int32, x.shape, 1)
    shift = 1
    while shift < x.shape[1]:
        x = x + jnp.where(lane >= shift, pltpu.roll(x, shift, 1), 0.0)
        shift *= 2
    return x


def kernel(
    n_seq, n_head, heads, blocks,
    q_hbm, k_hbm, v_hbm, gate_hbm, og_hbm, decay_ref, doc_ref, gain_ref,
    gated_ref, ggrad_ref, qgrad_ref, kgrad_ref, vgrad_ref,
    qb, kb, vb, gateb, ogb, in_sem,
    crow, passrow, cols, mask, wbuf, pbuf, attn, gbuf, keyed, qkeyed, agrad,
    local, blocal, held, bheld, acc, norm,
    fsend, frecv, fcarry, fin, bsend, brecv, bcarry, bin_, sums,
    f1s, f1r, f2s, f2r, b1s, b1r, b2s, b2r, hs, hr,
):
    seq = lax.axis_index("seq")
    hx = lax.axis_index("head")
    width = HEAD_TOTAL * HD

    barrier = pltpu.get_barrier_semaphore()

    def greet_seq(o, _):
        pl.semaphore_signal(barrier, inc=1, device_id={"seq": lax.rem(seq + o, n_seq)}, device_id_type=MESH)
        return 0

    def greet_head(o, _):
        pl.semaphore_signal(barrier, inc=1, device_id={"head": lax.rem(hx + o, n_head)}, device_id_type=MESH)
        return 0

    lax.fori_loop(1, n_seq, greet_seq, 0)
    lax.fori_loop(1, n_head, greet_head, 0)

    pairs = ((k_hbm, kb), (v_hbm, vb), (q_hbm, qb), (gate_hbm, gateb), (og_hbm, ogb))

    def load(i, h):
        src, dst = pairs[i]
        return pltpu.make_async_copy(
            src.at[:, pl.ds(pl.multiple_of(h * HD, HD), HD)], dst.at[h], in_sem.at[i, h]
        )

    def start_kv(h, _):
        load(0, h).start()
        load(1, h).start()
        return 0

    def start_rest(h, _):
        load(2, h).start()
        load(3, h).start()
        load(4, h).start()
        return 0

    lax.fori_loop(0, heads, start_kv, 0)
    lax.fori_loop(0, heads, start_rest, 0)

    doc = doc_ref[...].astype(F32)
    per = BLOCK // HD
    for b in range(blocks):
        flags = jnp.concatenate([doc[b * per + i : b * per + i + 1, :] for i in range(per)], axis=1)
        flags = jnp.broadcast_to(flags, (heads, BLOCK))
        c = running_sum(decay_ref[:, b * BLOCK : (b + 1) * BLOCK])
        r = running_sum(flags)
        c_last = c[:, BLOCK - 1 :]
        r_last = r[:, BLOCK - 1 :]
        enter = jnp.where(r == 0.0, jnp.exp(c), 0.0)
        leave = jnp.where(r == r_last, jnp.exp(c_last - c), 0.0)
        passing = jnp.where(r_last == 0.0, jnp.exp(c_last), 0.0)
        crow[b] = c
        passrow[b] = jnp.broadcast_to(passing, (heads, HD))
        hi, mid, low = pieces(jnp.concatenate([c, enter, leave, r], axis=0))
        stacked = jnp.concatenate([hi, mid, low, jnp.zeros_like(hi)], axis=0)
        cols[b] = stacked.T.astype(BF16)

    def pick(h, *quantities):
        row = lax.broadcasted_iota(jnp.int32, (HD, HD), 0)
        live = row < 96
        out = [
            jnp.where(live & ((row & 31) == quantity * 8 + h), 1.0, 0.0).astype(BF16)
            for quantity in quantities
        ]
        return jnp.concatenate(out, axis=1) if len(out) > 1 else out[0]

    def columns(b, h, *quantities):
        both = mm(cols[b], pick(h, *quantities))
        return [both[:, i * HD : (i + 1) * HD] for i in range(len(quantities))]

    def local_states(h, _):
        load(0, h).wait()
        load(1, h).wait()
        state = None
        for b in range(blocks):
            rows = pl.ds(b * BLOCK, BLOCK)
            (leave,) = columns(b, h, LEAVE)
            key = (kb[h, rows, :].astype(F32) * leave).astype(BF16)
            keyed[h, rows, :] = key
            part = mm(key, vb[h, rows, :], TN)
            local[b, h] = part
            state = part if state is None else passrow[b, pl.ds(h, 1), :] * state + part
        total = passrow[0, pl.ds(h, 1), :]
        for b in range(1, blocks):
            total = total * passrow[b, pl.ds(h, 1), :]
        for i in range(2):
            fsend[2 * h + i, 0:64, :] = state[64 * i : 64 * i + 64, :]
            fsend[2 * h + i, 64:72, :] = jnp.broadcast_to(total, (8, HD))
        return 0

    lax.fori_loop(0, heads, local_states, 0)

    pl.semaphore_wait(barrier, n_seq - 1 + n_head - 1)

    def exchange(src, dst, s_sem, r_sem, o):
        peer = lax.rem(seq + o, n_seq)
        return pltpu.make_async_remote_copy(
            src_ref=src.at[peer], dst_ref=dst.at[seq], send_sem=s_sem.at[o], recv_sem=r_sem.at[o],
            device_id={"seq": peer}, device_id_type=MESH,
        )

    def start_all(src, dst, s_sem, r_sem):
        def go(o, _):
            exchange(src, dst, s_sem, r_sem, o).start()
            return 0

        lax.fori_loop(1, n_seq, go, 0)

    def wait_all(src, dst, s_sem, r_sem):
        def go(o, _):
            exchange(src, dst, s_sem, r_sem, o).wait()
            return 0

        lax.fori_loop(1, n_seq, go, 0)

    f1 = (fsend, frecv, f1s, f1r)
    f2 = (fcarry, fin, f2s, f2r)
    b1 = (bsend, brecv, b1s, b1r)
    b2 = (bcarry, bin_, b2s, b2r)
    start_all(*f1)

    for b in range(blocks):
        (r_col,) = columns(b, 0, COUNT)
        flags = jnp.concatenate([doc[b * per + i : b * per + i + 1, :] for i in range(per)], axis=1)
        r_row = running_sum(jnp.broadcast_to(flags, (8, BLOCK)))[0:1, :]
        for i in range(BLOCK // HD):
            t = lax.broadcasted_iota(jnp.int32, (BLOCK, HD), 0)
            j = lax.broadcasted_iota(jnp.int32, (BLOCK, HD), 1) + i * HD
            same = r_col == r_row[:, i * HD : (i + 1) * HD]
            mask[b, :, i * HD : (i + 1) * HD] = jnp.where(same & (j <= t), jnp.inf, -jnp.inf)

    tiles = [(0, 0), (1, 0), (1, 1)]

    def inside_part(h, _):
        load(2, h).wait()
        for b in range(blocks):
            rows = pl.ds(b * BLOCK, BLOCK)
            cum, enter = columns(b, h, CUM, ENTER)
            query = qb[h, rows, :]
            qkeyed[h, rows, :] = (query.astype(F32) * enter).astype(BF16)
            row = crow[b, pl.ds(h, 1), :]
            out = [None, None]
            for index, (ti, tj) in enumerate(tiles):
                t = slice(ti * HALF, (ti + 1) * HALF)
                j = slice(tj * HALF, (tj + 1) * HALF)
                score = mm(query[t], kb[h, pl.ds(b * BLOCK + tj * HALF, HALF), :], NT)
                c_t = cum[t]
                diff = jnp.concatenate([c_t, c_t], axis=1) - row[:, j]
                w = jnp.exp(jnp.minimum(diff, mask[b, t, j]))
                prob = (score * w).astype(BF16)
                wbuf[h, b, index] = w.astype(BF16)
                pbuf[h, b, index] = prob
                part = mm(prob, vb[h, pl.ds(b * BLOCK + tj * HALF, HALF), :])
                out[ti] = part if out[ti] is None else out[ti] + part
            for ti in range(2):
                attn[h, pl.ds(b * BLOCK + ti * HALF, HALF), :] = out[ti]
        return 0

    lax.fori_loop(0, heads // 2, inside_part, 0)

    wait_all(*f1)
    frecv[seq] = fsend[seq]
    fcarry[0] = jnp.zeros((64, HD), F32)

    def advance(d, _):
        fcarry[d + 1] = frecv[d, 64:65, :] * fcarry[d] + frecv[d, 0:64, :]
        return 0

    lax.fori_loop(0, n_seq - 1, advance, 0)
    start_all(*f2)
    fin[seq] = fcarry[seq]

    lax.fori_loop(heads // 2, heads, inside_part, 0)

    def gate_part(h, _):
        load(3, h).wait()
        load(4, h).wait()
        sig = jax.nn.sigmoid(gateb[h].astype(F32))
        gbuf[h] = ogb[h].astype(F32) * sig * gain_ref[pl.ds(h, 1), :]
        return 0

    lax.fori_loop(0, heads, gate_part, 0)
    acc[...] = jnp.zeros_like(acc)

    wait_all(*f2)

    def outside_part(h, _):
        carry = fin[pl.ds(2 * h, 2)].reshape(HD, HD)
        for b in range(blocks):
            rows = pl.ds(b * BLOCK, BLOCK)
            state = carry.astype(BF16)
            held[b, h] = state
            out = attn[h, rows, :] + mm(qkeyed[h, rows, :], state)
            attn[h, rows, :] = out
            acc[0, rows, :] += out * out
            acc[1, rows, :] += out * gbuf[h, rows, :]
            if b + 1 < blocks:
                carry = passrow[b, pl.ds(h, 1), :] * carry + local[b, h]
        return 0

    lax.fori_loop(0, heads, outside_part, 0)

    parts = []
    for i in range(2):
        value = acc[i]
        hi = value.astype(BF16)
        parts += [hi, (value - hi.astype(F32)).astype(BF16)]
    row = lax.broadcasted_iota(jnp.int32, (8, 4 * HD), 0)
    lane = lax.broadcasted_iota(jnp.int32, (8, 4 * HD), 1)
    chooser = jnp.where((row < 4) == (lane < 2 * HD), 1.0, 0.0).astype(BF16)
    totals = mm(chooser, jnp.concatenate(parts, axis=1), NT)
    pieces_n = totals.shape[1] // HD
    sums[hx] = jnp.concatenate(
        [totals[r : r + 1, i * HD : (i + 1) * HD] for r in (0, 4) for i in range(pieces_n)], axis=0
    )

    def head_copy(o):
        peer = lax.rem(hx + o, n_head)
        return pltpu.make_async_remote_copy(
            src_ref=sums.at[hx], dst_ref=sums.at[hx], send_sem=hs.at[o], recv_sem=hr.at[o],
            device_id={"head": peer}, device_id_type=MESH,
        )

    def head_start(o, _):
        head_copy(o).start()
        return 0

    def head_wait(o, _):
        head_copy(o).wait()
        return 0

    lax.fori_loop(1, n_head, head_start, 0)
    lax.fori_loop(1, n_head, head_wait, 0)
    both = sums[0]
    for i in range(1, n_head):
        both = both + sums[i]
    inverse = lax.rsqrt(both[0:8, :] / width + EPSILON)
    coef = inverse * inverse * inverse * both[8:16, :] / width
    hi, mid, low = pieces(jnp.concatenate([inverse, coef, jnp.zeros((16, HD), F32)], axis=0))
    turned = jnp.concatenate([hi, mid, low, jnp.zeros_like(hi)], axis=0).T.astype(BF16)
    for i in range(8):
        wide = mm(turned, pick(i, 0, 1))
        norm[0, i * HD : (i + 1) * HD, :] = wide[:, :HD]
        norm[1, i * HD : (i + 1) * HD, :] = wide[:, HD:]

    def grad_part(h, _):
        state = None
        for b in reversed(range(blocks)):
            rows = pl.ds(b * BLOCK, BLOCK)
            ag = (norm[0, rows, :] * gbuf[h, rows, :] - attn[h, rows, :] * norm[1, rows, :]).astype(BF16)
            agrad[h, rows, :] = ag
            part = mm(qkeyed[h, rows, :], ag, TN)
            blocal[b, h] = part
            state = part if state is None else part + passrow[b, pl.ds(h, 1), :] * state
        bsend[2 * h] = state[0:64, :]
        bsend[2 * h + 1] = state[64:128, :]
        return 0

    lax.fori_loop(0, heads, grad_part, 0)
    start_all(*b1)

    def back_part(h, _):
        lanes = pl.ds(pl.multiple_of(h * HD, HD), HD)
        gain = gain_ref[pl.ds(h, 1), :]
        sig = jax.nn.sigmoid(gateb[h].astype(F32))
        gate = attn[h] * norm[0] * gain * sig
        gated_ref[:, lanes] = gate.astype(BF16)
        ggrad_ref[:, lanes] = (ogb[h].astype(F32) * gate * (1.0 - sig)).astype(BF16)
        for b in range(blocks):
            rows = pl.ds(b * BLOCK, BLOCK)
            (enter,) = columns(b, h, ENTER)
            query = qb[h, rows, :]
            key = kb[h, rows, :]
            value = vb[h, rows, :]
            ag = agrad[h, rows, :]
            qg = [None, None]
            kg = [None, None]
            vg = [None, None]
            for index, (ti, tj) in enumerate(tiles):
                t = slice(ti * HALF, (ti + 1) * HALF)
                j = slice(tj * HALF, (tj + 1) * HALF)
                ds = (mm(ag[t], value[j], NT) * wbuf[h, b, index].astype(F32)).astype(BF16)
                part = mm(ds, key[j])
                qg[ti] = part if qg[ti] is None else qg[ti] + part
                part = mm(ds, query[t], TN)
                kg[tj] = part if kg[tj] is None else kg[tj] + part
                part = mm(pbuf[h, b, index], ag[t], TN)
                vg[tj] = part if vg[tj] is None else vg[tj] + part
            outside = mm(ag, held[b, h], NT) * enter
            for i in range(2):
                here = pl.ds(b * BLOCK + i * HALF, HALF)
                qgrad_ref[here, lanes] = (qg[i] + outside[i * HALF : (i + 1) * HALF]).astype(BF16)
                attn[h, here, :] = kg[i]
                gbuf[h, here, :] = vg[i]
        return 0

    lax.fori_loop(0, heads // 2, back_part, 0)

    wait_all(*b1)
    brecv[seq] = bsend[seq]
    bcarry[n_seq - 1] = jnp.zeros((64, HD), F32)

    def retreat(i, _):
        d = n_seq - 1 - i
        bcarry[d - 1] = frecv[d, 64:65, :] * bcarry[d] + brecv[d]
        return 0

    lax.fori_loop(0, n_seq - 1, retreat, 0)
    start_all(*b2)
    bin_[seq] = bcarry[seq]

    lax.fori_loop(heads // 2, heads, back_part, 0)

    wait_all(*b2)

    def final_part(h, _):
        lanes = pl.ds(pl.multiple_of(h * HD, HD), HD)
        carry = bin_[pl.ds(2 * h, 2)].reshape(HD, HD)
        for b in reversed(range(blocks)):
            rows = pl.ds(b * BLOCK, BLOCK)
            (leave,) = columns(b, h, LEAVE)
            state = carry.astype(BF16)
            kgrad_ref[rows, lanes] = (
                attn[h, rows, :] + leave * mm(vb[h, rows, :], state, NT)
            ).astype(BF16)
            vgrad_ref[rows, lanes] = (gbuf[h, rows, :] + mm(keyed[h, rows, :], state)).astype(BF16)
            if b:
                carry = blocal[b, h] + passrow[b, pl.ds(h, 1), :] * carry
        return 0

    lax.fori_loop(0, heads, final_part, 0)


def solution(mesh):
    n_seq, n_head = mesh.shape["seq"], mesh.shape["head"]

    def body(queries, key_rows, value_rows, log_decay, doc_start, gate_input, norm_gain, out_grad):
        rows, width = queries.shape
        heads = width // HD
        blocks = rows // BLOCK
        whole = pl.BlockSpec(memory_space=pltpu.VMEM)
        hbm = pl.BlockSpec(memory_space=pl.ANY)
        dma = pltpu.SemaphoreType.DMA
        big = lambda kind: pltpu.VMEM((heads, rows, HD), kind)
        seq_sems = dma((n_seq,))
        outs = pl.pallas_call(
            functools.partial(kernel, n_seq, n_head, heads, blocks),
            name="lightning",
            out_shape=[pltpu.VMEM((rows, width), BF16)] * 5,
            in_specs=[hbm] * 5 + [whole] * 3,
            out_specs=[whole] * 5,
            scratch_shapes=[
                big(BF16), big(BF16), big(BF16), big(BF16), big(BF16), dma((5, heads)),
                pltpu.VMEM((blocks, heads, BLOCK), F32),
                pltpu.VMEM((blocks, heads, HD), F32),
                pltpu.VMEM((blocks, BLOCK, HD), BF16),
                pltpu.VMEM((blocks, BLOCK, BLOCK), F32),
                pltpu.VMEM((heads, blocks, 3, HALF, HALF), BF16),
                pltpu.VMEM((heads, blocks, 3, HALF, HALF), BF16),
                big(F32), big(F32), big(BF16), big(BF16), big(BF16),
                pltpu.VMEM((blocks, heads, HD, HD), F32),
                pltpu.VMEM((blocks, heads, HD, HD), F32),
                pltpu.VMEM((blocks, heads, HD, HD), BF16),
                pltpu.VMEM((8, HD), F32),
                pltpu.VMEM((2, rows, HD), F32),
                pltpu.VMEM((2, rows, HD), F32),
                pltpu.VMEM((n_seq, 72, HD), F32),
                pltpu.VMEM((n_seq, 72, HD), F32),
                pltpu.VMEM((n_seq, 64, HD), F32),
                pltpu.VMEM((n_seq, 64, HD), F32),
                pltpu.VMEM((n_seq, 64, HD), F32),
                pltpu.VMEM((n_seq, 64, HD), F32),
                pltpu.VMEM((n_seq, 64, HD), F32),
                pltpu.VMEM((n_seq, 64, HD), F32),
                pltpu.VMEM((n_head, 16, HD), F32),
                seq_sems, seq_sems, seq_sems, seq_sems, seq_sems, seq_sems, seq_sems, seq_sems,
                dma((n_head,)), dma((n_head,)),
            ],
            compiler_params=pltpu.CompilerParams(
                collective_id=0, has_side_effects=True, vmem_limit_bytes=50 << 20
            ),
        )(
            queries, key_rows, value_rows, gate_input, out_grad, log_decay,
            doc_start.reshape(8, HD), norm_gain.reshape(8, HD),
        )
        return tuple(outs)

    block = P("seq", "head")
    return jax.shard_map(
        body,
        mesh=mesh,
        in_specs=(block, block, block, P("head", "seq"), P("seq"), block, P("head"), block),
        out_specs=(block,) * 5,
        check_vma=False,
    )
```

time: 639 us -> 65.6 us (0.10); the launches traced: 629 us -> 65.5 us
  waiting for transfers between devices: 355 us -> 0 us
  starting transfers between devices: 108 us -> 0 us
  Pallas kernels: 0 us -> 58.2 us
  matrix products: 57.4 us -> 0 us
  other arithmetic: 52.7 us -> 0 us
  local copies, waits for them, and re-layouts: 41.6 us -> 6.6 us
  blocking collectives: 13.5 us -> 0 us
    ppermute x30 -> x0, waiting for transfers between devices: 355 us -> none  [passed_along(): return lax.ppermute(block, axis, route)]
    ppermute x30 -> x0, starting transfers between devices: 108 us -> none  [passed_along(): return lax.ppermute(block, axis, route)]
    pallas_call x0 -> x1, Pallas kernels: none -> 58.2 us  [body(): pl.pallas_call(functools.partial(kernel, n_seq, n_head, heads, blocks), n...]
    dot_general x12 -> x0, matrix products: 57.4 us -> none  [the longest x1 8.64 us: body(): jnp.einsum('nhts,nthe->nshe', weights_bf, agrad_block, preferred_element_...]
    add x32 -> x0, other arithmetic: 29.5 us -> none  [the longest x15 14.8 us: backward_advance(): return (arrived, dev_back + total_pass[:, None, None] * arrived)]
    psum x1 -> x0, blocking collectives: 13.5 us -> none  [body(): lax.psum((jnp.sum(attn * attn, axis=1), jnp.sum(gnorm * norm_gain[None, :...]
    convert_element_type x4 -> x0, local copies, waits for them, and re-layouts: 11.3 us -> none  [the longest x2 6.05 us: body(): value_grad = vgrad.reshape(row_count, width_dev).astype(jnp.bfloat16)]
    another operation x6 -> x0, other arithmetic: 9.41 us -> none
  transfers between devices with their start and end apart: 30 -> 0, of which waited for: 30 -> 0; matrix products, arithmetic and copies ran while one was open for 0% -> 0% of each run, Pallas kernels for 0% -> 0%
where the time goes in v1:
time: 65.6 us; the launch traced here: 65.5 us
  Pallas kernels  58.2 us (89%)
  local copies, waits for them, and re-layouts  6.6 us (10%)
    pallas_call x1, Pallas kernels, body(): pl.pallas_call(functools.partial(kernel, n_seq, n_head, heads, blocks), n...  58.2 us
    unnamed x5, local copies, waits for them, and re-layouts  6.6 us

profile of v1, /device:TPU:0, one launch (start us, length us, event | category | flops | bytes accessed | tf_op | source)
XLA Modules:
  0.0 65.5 jit_solution(17196608623627904101)
XLA Ops:
  0.6 58.2 %lightning.1 = (bf16[1024,1024]{1,0:T(8,128)(2,1)S(1)}, bf16[1024,1024]{1,0:T(8,128)(2,1)S(1)}, bf16[1024,1024]{1,0:T(8,128)(2,1)S(1)}, bf16[1024,1024]{1,0:T(8,128)(2,1)S(1)}, bf16[1024,1024]{1,0:T(8,128)(2,1)S(1)}) custom-call(bf16[1024,1024]{1,0:T(8,128)(2,1)} %q_hbm.1, bf16[1024,1024]{1,0:T(8,128)(2,1)} %k_hbm.1, bf16[1024,1024]{1,0:T(8,128)(2,1)} %v_hbm.1, ...), custom_call_target="tpu_custom_call" | custom-call | tf_op jit(solution)/shard_map/lightning/pallas_call | solution.py:402
  58.9 1.3 %copy.18 = bf16[1024,1024]{1,0:T(8,128)(2,1)} copy(bf16[1024,1024]{1,0:T(8,128)(2,1)S(1)} %get-tuple-element.5) | data formatting | bytes 4194304
  60.2 1.3 %copy.19 = bf16[1024,1024]{1,0:T(8,128)(2,1)} copy(bf16[1024,1024]{1,0:T(8,128)(2,1)S(1)} %get-tuple-element.6) | data formatting | bytes 4194304
  61.5 1.3 %copy.20 = bf16[1024,1024]{1,0:T(8,128)(2,1)} copy(bf16[1024,1024]{1,0:T(8,128)(2,1)S(1)} %get-tuple-element.7) | data formatting | bytes 4194304
  62.8 1.3 %copy.21 = bf16[1024,1024]{1,0:T(8,128)(2,1)} copy(bf16[1024,1024]{1,0:T(8,128)(2,1)S(1)} %get-tuple-element.8) | data formatting | bytes 4194304
  64.1 1.3 %copy.22 = bf16[1024,1024]{1,0:T(8,128)(2,1)} copy(bf16[1024,1024]{1,0:T(8,128)(2,1)S(1)} %get-tuple-element.9) | data formatting | bytes 4194304

commit v2 on v1

--- a/solution.py
+++ b/solution.py
@@ -12,6 +12,9 @@
 BLOCK = 512
 HALF = 256
 EPSILON = 1e-06
+GROUPS = 2
+SPLIT_F = 4
+SPLIT_B = 4
 MESH = pl.DeviceIdType.MESH
 F32 = jnp.float32
 BF16 = jnp.bfloat16
@@ -45,18 +48,20 @@
 
 
 def kernel(
-    n_seq, n_head, heads, blocks,
-    q_hbm, k_hbm, v_hbm, gate_hbm, og_hbm, decay_ref, doc_ref, gain_ref,
+    n_seq, n_head, heads, blocks, groups,
+    q_hbm, k_hbm, v_hbm, gate_hbm, og_hbm, decay_hbm, doc_hbm, gain_hbm,
     gated_ref, ggrad_ref, qgrad_ref, kgrad_ref, vgrad_ref,
-    qb, kb, vb, gateb, ogb, in_sem,
+    qb, kb, vb, gateb, ogb, in_sem, decay_ref, doc_ref, gain_ref, small_sem,
     crow, passrow, cols, mask, wbuf, pbuf, attn, gbuf, keyed, qkeyed, agrad,
-    local, blocal, held, bheld, acc, norm,
-    fsend, frecv, fcarry, fin, bsend, brecv, bcarry, bin_, sums,
-    f1s, f1r, f2s, f2r, b1s, b1r, b2s, b2r, hs, hr,
+    local, blocal, held, acc, norm,
+    passall, fsend, frecv, fcarry, fin, bsend, brecv, bcarry, bin_, sums,
+    ps, pr, f1s, f1r, f2s, f2r, b1s, b1r, b2s, b2r, hs, hr,
 ):
     seq = lax.axis_index("seq")
     hx = lax.axis_index("head")
     width = HEAD_TOTAL * HD
+    team = heads // groups
+    band = HD // n_seq
 
     barrier = pltpu.get_barrier_semaphore()
 
@@ -68,9 +73,12 @@
         pl.semaphore_signal(barrier, inc=1, device_id={"head": lax.rem(hx + o, n_head)}, device_id_type=MESH)
         return 0
 
-    lax.fori_loop(1, n_seq, greet_seq, 0)
-    lax.fori_loop(1, n_head, greet_head, 0)
-
+    small = [
+        pltpu.make_async_copy(src, dst, small_sem.at[i])
+        for i, (src, dst) in enumerate(((decay_hbm, decay_ref), (doc_hbm, doc_ref), (gain_hbm, gain_ref)))
+    ]
+    for copy in small:
+        copy.start()
     pairs = ((k_hbm, kb), (v_hbm, vb), (q_hbm, qb), (gate_hbm, gateb), (og_hbm, ogb))
 
     def load(i, h):
@@ -84,17 +92,25 @@
         load(1, h).start()
         return 0
 
-    def start_rest(h, _):
-        load(2, h).start()
-        load(3, h).start()
-        load(4, h).start()
-        return 0
+    def start_rest(i):
+        def go(h, _):
+            load(i, h).start()
+            return 0
+
+        return go
 
     lax.fori_loop(0, heads, start_kv, 0)
-    lax.fori_loop(0, heads, start_rest, 0)
+    lax.fori_loop(1, n_seq, greet_seq, 0)
+    lax.fori_loop(1, n_head, greet_head, 0)
+    lax.fori_loop(0, heads, start_rest(2), 0)
+    lax.fori_loop(0, heads, start_rest(3), 0)
+    lax.fori_loop(0, heads, start_rest(4), 0)
+    for copy in small:
+        copy.wait()
 
     doc = doc_ref[...].astype(F32)
     per = BLOCK // HD
+    total = None
     for b in range(blocks):
         flags = jnp.concatenate([doc[b * per + i : b * per + i + 1, :] for i in range(per)], axis=1)
         flags = jnp.broadcast_to(flags, (heads, BLOCK))
@@ -105,11 +121,33 @@
         enter = jnp.where(r == 0.0, jnp.exp(c), 0.0)
         leave = jnp.where(r == r_last, jnp.exp(c_last - c), 0.0)
         passing = jnp.where(r_last == 0.0, jnp.exp(c_last), 0.0)
+        passing = jnp.broadcast_to(passing, (heads, HD))
         crow[b] = c
-        passrow[b] = jnp.broadcast_to(passing, (heads, HD))
+        passrow[b] = passing
+        total = passing if total is None else total * passing
         hi, mid, low = pieces(jnp.concatenate([c, enter, leave, r], axis=0))
         stacked = jnp.concatenate([hi, mid, low, jnp.zeros_like(hi)], axis=0)
         cols[b] = stacked.T.astype(BF16)
+    passall[seq] = total
+
+    pl.semaphore_wait(barrier, n_seq - 1 + n_head - 1)
+
+    def pass_copy(o):
+        peer = lax.rem(seq + o, n_seq)
+        return pltpu.make_async_remote_copy(
+            src_ref=passall.at[seq], dst_ref=passall.at[seq], send_sem=ps.at[o], recv_sem=pr.at[o],
+            device_id={"seq": peer}, device_id_type=MESH,
+        )
+
+    def pass_start(o, _):
+        pass_copy(o).start()
+        return 0
+
+    def pass_wait(o, _):
+        pass_copy(o).wait()
+        return 0
+
+    lax.fori_loop(1, n_seq, pass_start, 0)
 
     def pick(h, *quantities):
         row = lax.broadcasted_iota(jnp.int32, (HD, HD), 0)
@@ -124,56 +162,67 @@
         both = mm(cols[b], pick(h, *quantities))
         return [both[:, i * HD : (i + 1) * HD] for i in range(len(quantities))]
 
-    def local_states(h, _):
-        load(0, h).wait()
-        load(1, h).wait()
-        state = None
-        for b in range(blocks):
-            rows = pl.ds(b * BLOCK, BLOCK)
-            (leave,) = columns(b, h, LEAVE)
-            key = (kb[h, rows, :].astype(F32) * leave).astype(BF16)
-            keyed[h, rows, :] = key
-            part = mm(key, vb[h, rows, :], TN)
-            local[b, h] = part
-            state = part if state is None else passrow[b, pl.ds(h, 1), :] * state + part
-        total = passrow[0, pl.ds(h, 1), :]
-        for b in range(1, blocks):
-            total = total * passrow[b, pl.ds(h, 1), :]
-        for i in range(2):
-            fsend[2 * h + i, 0:64, :] = state[64 * i : 64 * i + 64, :]
-            fsend[2 * h + i, 64:72, :] = jnp.broadcast_to(total, (8, HD))
-        return 0
-
-    lax.fori_loop(0, heads, local_states, 0)
-
-    pl.semaphore_wait(barrier, n_seq - 1 + n_head - 1)
-
-    def exchange(src, dst, s_sem, r_sem, o):
+    def exchange(g, src, dst, s_sem, r_sem, o):
         peer = lax.rem(seq + o, n_seq)
         return pltpu.make_async_remote_copy(
-            src_ref=src.at[peer], dst_ref=dst.at[seq], send_sem=s_sem.at[o], recv_sem=r_sem.at[o],
+            src_ref=src.at[g, peer], dst_ref=dst.at[g, seq], send_sem=s_sem.at[g, o], recv_sem=r_sem.at[g, o],
             device_id={"seq": peer}, device_id_type=MESH,
         )
 
-    def start_all(src, dst, s_sem, r_sem):
+    def start_all(g, src, dst, s_sem, r_sem):
         def go(o, _):
-            exchange(src, dst, s_sem, r_sem, o).start()
+            exchange(g, src, dst, s_sem, r_sem, o).start()
             return 0
 
         lax.fori_loop(1, n_seq, go, 0)
 
-    def wait_all(src, dst, s_sem, r_sem):
+    def wait_all(g, src, dst, s_sem, r_sem):
         def go(o, _):
-            exchange(src, dst, s_sem, r_sem, o).wait()
+            exchange(g, src, dst, s_sem, r_sem, o).wait()
             return 0
 
         lax.fori_loop(1, n_seq, go, 0)
+
+    def put_bands(ref, g, h, state):
+        place = pl.ds(pl.multiple_of((h - g * team) * band, band), band)
+        ref[g, :, place, :] = state.reshape(n_seq, band, HD)
+
+    def get_bands(ref, g, h):
+        place = pl.ds(pl.multiple_of((h - g * team) * band, band), band)
+        return ref[g, :, place, :].reshape(HD, HD)
+
+    def pass_bands(d, g):
+        return jnp.concatenate(
+            [jnp.broadcast_to(passall[d, g * team + i : g * team + i + 1, :], (band, HD)) for i in range(team)],
+            axis=0,
+        )
 
     f1 = (fsend, frecv, f1s, f1r)
     f2 = (fcarry, fin, f2s, f2r)
     b1 = (bsend, brecv, b1s, b1r)
     b2 = (bcarry, bin_, b2s, b2r)
-    start_all(*f1)
+
+    def local_states(g):
+        def go(h, _):
+            load(0, h).wait()
+            load(1, h).wait()
+            state = None
+            for b in range(blocks):
+                rows = pl.ds(b * BLOCK, BLOCK)
+                (leave,) = columns(b, h, LEAVE)
+                key = (kb[h, rows, :].astype(F32) * leave).astype(BF16)
+                keyed[h, rows, :] = key
+                part = mm(key, vb[h, rows, :], TN)
+                local[b, h] = part
+                state = part if state is None else passrow[b, pl.ds(h, 1), :] * state + part
+            put_bands(fsend, g, h, state)
+            return 0
+
+        return go
+
+    for g in range(groups):
+        lax.fori_loop(g * team, (g + 1) * team, local_states(g), 0)
+        start_all(g, *f1)
 
     for b in range(blocks):
         (r_col,) = columns(b, 0, COUNT)
@@ -212,21 +261,24 @@
                 attn[h, pl.ds(b * BLOCK + ti * HALF, HALF), :] = out[ti]
         return 0
 
-    lax.fori_loop(0, heads // 2, inside_part, 0)
-
-    wait_all(*f1)
-    frecv[seq] = fsend[seq]
-    fcarry[0] = jnp.zeros((64, HD), F32)
-
-    def advance(d, _):
-        fcarry[d + 1] = frecv[d, 64:65, :] * fcarry[d] + frecv[d, 0:64, :]
-        return 0
-
-    lax.fori_loop(0, n_seq - 1, advance, 0)
-    start_all(*f2)
-    fin[seq] = fcarry[seq]
-
-    lax.fori_loop(heads // 2, heads, inside_part, 0)
+    lax.fori_loop(0, SPLIT_F, inside_part, 0)
+
+    lax.fori_loop(1, n_seq, pass_wait, 0)
+    for g in range(groups):
+        wait_all(g, *f1)
+        frecv[g, seq] = fsend[g, seq]
+        fcarry[g, 0] = jnp.zeros((team * band, HD), F32)
+
+        def advance(d, carry):
+            carry = pass_bands(d, g) * carry + frecv[g, d]
+            fcarry[g, d + 1] = carry
+            return carry
+
+        lax.fori_loop(0, n_seq - 1, advance, jnp.zeros((team * band, HD), F32))
+        start_all(g, *f2)
+        fin[g, seq] = fcarry[g, seq]
+
+    lax.fori_loop(SPLIT_F, heads, inside_part, 0)
 
     def gate_part(h, _):
         load(3, h).wait()
@@ -238,23 +290,26 @@
     lax.fori_loop(0, heads, gate_part, 0)
     acc[...] = jnp.zeros_like(acc)
 
-    wait_all(*f2)
-
-    def outside_part(h, _):
-        carry = fin[pl.ds(2 * h, 2)].reshape(HD, HD)
-        for b in range(blocks):
-            rows = pl.ds(b * BLOCK, BLOCK)
-            state = carry.astype(BF16)
-            held[b, h] = state
-            out = attn[h, rows, :] + mm(qkeyed[h, rows, :], state)
-            attn[h, rows, :] = out
-            acc[0, rows, :] += out * out
-            acc[1, rows, :] += out * gbuf[h, rows, :]
-            if b + 1 < blocks:
-                carry = passrow[b, pl.ds(h, 1), :] * carry + local[b, h]
-        return 0
-
-    lax.fori_loop(0, heads, outside_part, 0)
+    def outside_part(g):
+        def go(h, _):
+            carry = get_bands(fin, g, h)
+            for b in range(blocks):
+                rows = pl.ds(b * BLOCK, BLOCK)
+                state = carry.astype(BF16)
+                held[b, h] = state
+                out = attn[h, rows, :] + mm(qkeyed[h, rows, :], state)
+                attn[h, rows, :] = out
+                acc[0, rows, :] += out * out
+                acc[1, rows, :] += out * gbuf[h, rows, :]
+                if b + 1 < blocks:
+                    carry = passrow[b, pl.ds(h, 1), :] * carry + local[b, h]
+            return 0
+
+        return go
+
+    for g in range(groups):
+        wait_all(g, *f2)
+        lax.fori_loop(g * team, (g + 1) * team, outside_part(g), 0, unroll=4)
 
     parts = []
     for i in range(2):
@@ -299,21 +354,24 @@
         norm[0, i * HD : (i + 1) * HD, :] = wide[:, :HD]
         norm[1, i * HD : (i + 1) * HD, :] = wide[:, HD:]
 
-    def grad_part(h, _):
-        state = None
-        for b in reversed(range(blocks)):
-            rows = pl.ds(b * BLOCK, BLOCK)
-            ag = (norm[0, rows, :] * gbuf[h, rows, :] - attn[h, rows, :] * norm[1, rows, :]).astype(BF16)
-            agrad[h, rows, :] = ag
-            part = mm(qkeyed[h, rows, :], ag, TN)
-            blocal[b, h] = part
-            state = part if state is None else part + passrow[b, pl.ds(h, 1), :] * state
-        bsend[2 * h] = state[0:64, :]
-        bsend[2 * h + 1] = state[64:128, :]
-        return 0
-
-    lax.fori_loop(0, heads, grad_part, 0)
-    start_all(*b1)
+    def grad_part(g):
+        def go(h, _):
+            state = None
+            for b in reversed(range(blocks)):
+                rows = pl.ds(b * BLOCK, BLOCK)
+                ag = (norm[0, rows, :] * gbuf[h, rows, :] - attn[h, rows, :] * norm[1, rows, :]).astype(BF16)
+                agrad[h, rows, :] = ag
+                part = mm(qkeyed[h, rows, :], ag, TN)
+                blocal[b, h] = part
+                state = part if state is None else part + passrow[b, pl.ds(h, 1), :] * state
+            put_bands(bsend, g, h, state)
+            return 0
+
+        return go
+
+    for g in range(groups):
+        lax.fori_loop(g * team, (g + 1) * team, grad_part(g), 0, unroll=4)
+        start_all(g, *b1)
 
     def back_part(h, _):
         lanes = pl.ds(pl.multiple_of(h * HD, HD), HD)
@@ -350,41 +408,56 @@
                 gbuf[h, here, :] = vg[i]
         return 0
 
-    lax.fori_loop(0, heads // 2, back_part, 0)
-
-    wait_all(*b1)
-    brecv[seq] = bsend[seq]
-    bcarry[n_seq - 1] = jnp.zeros((64, HD), F32)
-
-    def retreat(i, _):
-        d = n_seq - 1 - i
-        bcarry[d - 1] = frecv[d, 64:65, :] * bcarry[d] + brecv[d]
-        return 0
-
-    lax.fori_loop(0, n_seq - 1, retreat, 0)
-    start_all(*b2)
-    bin_[seq] = bcarry[seq]
-
-    lax.fori_loop(heads // 2, heads, back_part, 0)
-
-    wait_all(*b2)
-
-    def final_part(h, _):
-        lanes = pl.ds(pl.multiple_of(h * HD, HD), HD)
-        carry = bin_[pl.ds(2 * h, 2)].reshape(HD, HD)
-        for b in reversed(range(blocks)):
-            rows = pl.ds(b * BLOCK, BLOCK)
-            (leave,) = columns(b, h, LEAVE)
-            state = carry.astype(BF16)
-            kgrad_ref[rows, lanes] = (
-                attn[h, rows, :] + leave * mm(vb[h, rows, :], state, NT)
-            ).astype(BF16)
-            vgrad_ref[rows, lanes] = (gbuf[h, rows, :] + mm(keyed[h, rows, :], state)).astype(BF16)
-            if b:
-                carry = blocal[b, h] + passrow[b, pl.ds(h, 1), :] * carry
-        return 0
-
-    lax.fori_loop(0, heads, final_part, 0)
+    lax.fori_loop(0, SPLIT_B, back_part, 0)
+
+    for g in range(groups):
+        wait_all(g, *b1)
+        brecv[g, seq] = bsend[g, seq]
+        bcarry[g, n_seq - 1] = jnp.zeros((team * band, HD), F32)
+
+        def retreat(i, carry):
+            d = n_seq - 1 - i
+            carry = pass_bands(d, g) * carry + brecv[g, d]
+            bcarry[g, d - 1] = carry
+            return carry
+
+        lax.fori_loop(0, n_seq - 1, retreat, jnp.zeros((team * band, HD), F32))
+        start_all(g, *b2)
+        bin_[g, seq] = bcarry[g, seq]
+
+    lax.fori_loop(SPLIT_B, heads, back_part, 0)
+
+    def final_part(g):
+        def go(h, _):
+            lanes = pl.ds(pl.multiple_of(h * HD, HD), HD)
+            carry = get_bands(bin_, g, h)
+            for b in reversed(range(blocks)):
+                rows = pl.ds(b * BLOCK, BLOCK)
+                (leave,) = columns(b, h, LEAVE)
+                state = carry.astype(BF16)
+                kgrad_ref[rows, lanes] = (
+                    attn[h, rows, :] + leave * mm(vb[h, rows, :], state, NT)
+                ).astype(BF16)
+                vgrad_ref[rows, lanes] = (gbuf[h, rows, :] + mm(keyed[h, rows, :], state)).astype(BF16)
+                if b:
+                    carry = blocal[b, h] + passrow[b, pl.ds(h, 1), :] * carry
+            return 0
+
+        return go
+
+    for g in range(groups):
+        wait_all(g, *b2)
+        lax.fori_loop(g * team, (g + 1) * team, final_part(g), 0, unroll=4)
+
+
+def deliver(*refs):
+    count = len(refs) // 2
+    sems = refs[-1]
+    copies = [pltpu.make_async_copy(refs[i], refs[count + i], sems.at[i]) for i in range(count)]
+    for copy in copies:
+        copy.start()
+    for copy in copies:
+        copy.wait()
 
 
 def solution(mesh):
@@ -394,19 +467,26 @@
         rows, width = queries.shape
         heads = width // HD
         blocks = rows // BLOCK
+        team = heads // GROUPS
+        band = HD // n_seq
         whole = pl.BlockSpec(memory_space=pltpu.VMEM)
         hbm = pl.BlockSpec(memory_space=pl.ANY)
         dma = pltpu.SemaphoreType.DMA
         big = lambda kind: pltpu.VMEM((heads, rows, HD), kind)
-        seq_sems = dma((n_seq,))
+        states = pltpu.VMEM((GROUPS, n_seq, team * band, HD), F32)
+        seq_sems = dma((GROUPS, n_seq))
         outs = pl.pallas_call(
-            functools.partial(kernel, n_seq, n_head, heads, blocks),
+            functools.partial(kernel, n_seq, n_head, heads, blocks, GROUPS),
             name="lightning",
             out_shape=[pltpu.VMEM((rows, width), BF16)] * 5,
-            in_specs=[hbm] * 5 + [whole] * 3,
+            in_specs=[hbm] * 8,
             out_specs=[whole] * 5,
             scratch_shapes=[
                 big(BF16), big(BF16), big(BF16), big(BF16), big(BF16), dma((5, heads)),
+                pltpu.VMEM((heads, rows), F32),
+                pltpu.VMEM((8, HD), jnp.int32),
+                pltpu.VMEM((8, HD), F32),
+                dma((3,)),
                 pltpu.VMEM((blocks, heads, BLOCK), F32),
                 pltpu.VMEM((blocks, heads, HD), F32),
                 pltpu.VMEM((blocks, BLOCK, HD), BF16),
@@ -417,18 +497,12 @@
                 pltpu.VMEM((blocks, heads, HD, HD), F32),
                 pltpu.VMEM((blocks, heads, HD, HD), F32),
                 pltpu.VMEM((blocks, heads, HD, HD), BF16),
-                pltpu.VMEM((8, HD), F32),
                 pltpu.VMEM((2, rows, HD), F32),
                 pltpu.VMEM((2, rows, HD), F32),
-                pltpu.VMEM((n_seq, 72, HD), F32),
-                pltpu.VMEM((n_seq, 72, HD), F32),
-                pltpu.VMEM((n_seq, 64, HD), F32),
-                pltpu.VMEM((n_seq, 64, HD), F32),
-                pltpu.VMEM((n_seq, 64, HD), F32),
-                pltpu.VMEM((n_seq, 64, HD), F32),
-                pltpu.VMEM((n_seq, 64, HD), F32),
-                pltpu.VMEM((n_seq, 64, HD), F32),
+                pltpu.VMEM((n_seq, heads, HD), F32),
+                states, states, states, states, states, states, states, states,
                 pltpu.VMEM((n_head, 16, HD), F32),
+                dma((n_seq,)), dma((n_seq,)),
                 seq_sems, seq_sems, seq_sems, seq_sems, seq_sems, seq_sems, seq_sems, seq_sems,
                 dma((n_head,)), dma((n_head,)),
             ],
@@ -439,7 +513,17 @@
             queries, key_rows, value_rows, gate_input, out_grad, log_decay,
             doc_start.reshape(8, HD), norm_gain.reshape(8, HD),
         )
-        return tuple(outs)
+        return tuple(
+            pl.pallas_call(
+                deliver,
+                name="deliver",
+                out_shape=[jax.ShapeDtypeStruct((rows, width), BF16)] * 5,
+                in_specs=[whole] * 5,
+                out_specs=[hbm] * 5,
+                scratch_shapes=[dma((5,))],
+                compiler_params=pltpu.CompilerParams(vmem_limit_bytes=1 << 20),
+            )(*[pltpu.with_memory_space_constraint(out, pltpu.VMEM) for out in outs])
+        )
 
     block = P("seq", "head")
     return jax.shard_map(

time: 65.6 us -> 57.8 us (0.88)
  local copies, waits for them, and re-layouts: 6.6 us -> 0 us
  Pallas kernels: 58.2 us -> 56.5 us
    unnamed x5 -> x0, local copies, waits for them, and re-layouts: 6.6 us -> none
    pallas_call x1 -> x2, Pallas kernels: 58.2 us -> 56.5 us  [the longest x1 52.5 us: body(): pl.pallas_call(functools.partial(kernel, n_seq, n_head, heads, blocks, GR...]
where the time goes in v2:
time: 57.8 us; the launch traced here: 57.1 us
  Pallas kernels  56.5 us (98%)
  between operations  0.64 us (1%)
    pallas_call x1, Pallas kernels, body(): pl.pallas_call(functools.partial(kernel, n_seq, n_head, heads, blocks, GR...  52.5 us
    pallas_call x1, Pallas kernels, body(): pl.pallas_call(deliver, name='deliver', out_shape=[jax.ShapeDtypeStruct((...  4.01 us

profile of v2, /device:TPU:0, one launch (start us, length us, event | category | flops | bytes accessed | tf_op | source)
XLA Modules:
  0.0 57.1 jit_solution(13355864537879808741)
XLA Ops:
  0.6 52.5 %lightning.1 = (bf16[1024,1024]{1,0:T(8,128)(2,1)S(1)}, bf16[1024,1024]{1,0:T(8,128)(2,1)S(1)}, bf16[1024,1024]{1,0:T(8,128)(2,1)S(1)}, bf16[1024,1024]{1,0:T(8,128)(2,1)S(1)}, bf16[1024,1024]{1,0:T(8,128)(2,1)S(1)}) custom-call(bf16[1024,1024]{1,0:T(8,128)(2,1)} %q_hbm.1, bf16[1024,1024]{1,0:T(8,128)(2,1)} %k_hbm.1, bf16[1024,1024]{1,0:T(8,128)(2,1)} %v_hbm.1, ...), custom_call_target="tpu_custom_call" | custom-call | tf_op jit(solution)/shard_map/lightning/pallas_call | solution.py:478
  53.1 4.0 %deliver.1 = (bf16[1024,1024]{1,0:T(8,128)(2,1)}, bf16[1024,1024]{1,0:T(8,128)(2,1)}, bf16[1024,1024]{1,0:T(8,128)(2,1)}, bf16[1024,1024]{1,0:T(8,128)(2,1)}, bf16[1024,1024]{1,0:T(8,128)(2,1)}) custom-call(bf16[1024,1024]{1,0:T(8,128)(2,1)S(1)} %get-tuple-element.10.refs_0_, bf16[1024,1024]{1,0:T(8,128)(2,1)S(1)} %get-tuple-element.11.refs_1_, ...), custom_call_target="tpu_custom_call" | custom-call | tf_op jit(solution)/shard_map/deliver/pallas_call | solution.py:517

commit v3 on v2

--- a/solution.py
+++ b/solution.py
@@ -13,8 +13,9 @@
 HALF = 256
 EPSILON = 1e-06
 GROUPS = 2
-SPLIT_F = 4
-SPLIT_B = 4
+SPLIT_F = (4, 4)
+SPLIT_B = (4, 4)
+UNROLL = True
 MESH = pl.DeviceIdType.MESH
 F32 = jnp.float32
 BF16 = jnp.bfloat16
@@ -144,7 +145,11 @@
         return 0
 
     def pass_wait(o, _):
-        pass_copy(o).wait()
+        pass_copy(o).wait_recv()
+        return 0
+
+    def pass_sent(o, _):
+        pass_copy(o).wait_send()
         return 0
 
     lax.fori_loop(1, n_seq, pass_start, 0)
@@ -174,11 +179,18 @@
             exchange(g, src, dst, s_sem, r_sem, o).start()
             return 0
 
-        lax.fori_loop(1, n_seq, go, 0)
+        lax.fori_loop(1, n_seq, go, 0, unroll=UNROLL)
 
     def wait_all(g, src, dst, s_sem, r_sem):
         def go(o, _):
-            exchange(g, src, dst, s_sem, r_sem, o).wait()
+            exchange(g, src, dst, s_sem, r_sem, o).wait_recv()
+            return 0
+
+        lax.fori_loop(1, n_seq, go, 0, unroll=UNROLL)
+
+    def sent_all(g, src, dst, s_sem, r_sem):
+        def go(o, _):
+            exchange(g, src, dst, s_sem, r_sem, o).wait_send()
             return 0
 
         lax.fori_loop(1, n_seq, go, 0)
@@ -261,10 +273,11 @@
                 attn[h, pl.ds(b * BLOCK + ti * HALF, HALF), :] = out[ti]
         return 0
 
-    lax.fori_loop(0, SPLIT_F, inside_part, 0)
-
+    lax.fori_loop(0, SPLIT_F[0], inside_part, 0)
     lax.fori_loop(1, n_seq, pass_wait, 0)
     for g in range(groups):
+        if g:
+            lax.fori_loop(SPLIT_F[g - 1], SPLIT_F[g], inside_part, 0)
         wait_all(g, *f1)
         frecv[g, seq] = fsend[g, seq]
         fcarry[g, 0] = jnp.zeros((team * band, HD), F32)
@@ -278,7 +291,7 @@
         start_all(g, *f2)
         fin[g, seq] = fcarry[g, seq]
 
-    lax.fori_loop(SPLIT_F, heads, inside_part, 0)
+    lax.fori_loop(SPLIT_F[-1], heads, inside_part, 0)
 
     def gate_part(h, _):
         load(3, h).wait()
@@ -337,11 +350,15 @@
         return 0
 
     def head_wait(o, _):
-        head_copy(o).wait()
-        return 0
-
-    lax.fori_loop(1, n_head, head_start, 0)
-    lax.fori_loop(1, n_head, head_wait, 0)
+        head_copy(o).wait_recv()
+        return 0
+
+    def head_sent(o, _):
+        head_copy(o).wait_send()
+        return 0
+
+    lax.fori_loop(1, n_head, head_start, 0, unroll=UNROLL)
+    lax.fori_loop(1, n_head, head_wait, 0, unroll=UNROLL)
     both = sums[0]
     for i in range(1, n_head):
         both = both + sums[i]
@@ -373,6 +390,8 @@
         lax.fori_loop(g * team, (g + 1) * team, grad_part(g), 0, unroll=4)
         start_all(g, *b1)
 
+    vkeyed = qkeyed
+
     def back_part(h, _):
         lanes = pl.ds(pl.multiple_of(h * HD, HD), HD)
         gain = gain_ref[pl.ds(h, 1), :]
@@ -382,11 +401,13 @@
         ggrad_ref[:, lanes] = (ogb[h].astype(F32) * gate * (1.0 - sig)).astype(BF16)
         for b in range(blocks):
             rows = pl.ds(b * BLOCK, BLOCK)
-            (enter,) = columns(b, h, ENTER)
+            enter, leave = columns(b, h, ENTER, LEAVE)
             query = qb[h, rows, :]
             key = kb[h, rows, :]
             value = vb[h, rows, :]
+            vkeyed[h, rows, :] = (value.astype(F32) * leave).astype(BF16)
             ag = agrad[h, rows, :]
+            query_t, ag_t = query.T, ag.T
             qg = [None, None]
             kg = [None, None]
             vg = [None, None]
@@ -396,21 +417,22 @@
                 ds = (mm(ag[t], value[j], NT) * wbuf[h, b, index].astype(F32)).astype(BF16)
                 part = mm(ds, key[j])
                 qg[ti] = part if qg[ti] is None else qg[ti] + part
-                part = mm(ds, query[t], TN)
+                part = mm(query_t[:, t], ds)
                 kg[tj] = part if kg[tj] is None else kg[tj] + part
-                part = mm(pbuf[h, b, index], ag[t], TN)
+                part = mm(ag_t[:, t], pbuf[h, b, index])
                 vg[tj] = part if vg[tj] is None else vg[tj] + part
             outside = mm(ag, held[b, h], NT) * enter
             for i in range(2):
                 here = pl.ds(b * BLOCK + i * HALF, HALF)
                 qgrad_ref[here, lanes] = (qg[i] + outside[i * HALF : (i + 1) * HALF]).astype(BF16)
-                attn[h, here, :] = kg[i]
-                gbuf[h, here, :] = vg[i]
-        return 0
-
-    lax.fori_loop(0, SPLIT_B, back_part, 0)
-
-    for g in range(groups):
+                attn[h, here, :] = kg[i].T
+                gbuf[h, here, :] = vg[i].T
+        return 0
+
+    lax.fori_loop(0, SPLIT_B[0], back_part, 0)
+    for g in range(groups):
+        if g:
+            lax.fori_loop(SPLIT_B[g - 1], SPLIT_B[g], back_part, 0)
         wait_all(g, *b1)
         brecv[g, seq] = bsend[g, seq]
         bcarry[g, n_seq - 1] = jnp.zeros((team * band, HD), F32)
@@ -425,7 +447,7 @@
         start_all(g, *b2)
         bin_[g, seq] = bcarry[g, seq]
 
-    lax.fori_loop(SPLIT_B, heads, back_part, 0)
+    lax.fori_loop(SPLIT_B[-1], heads, back_part, 0)
 
     def final_part(g):
         def go(h, _):
@@ -433,11 +455,8 @@
             carry = get_bands(bin_, g, h)
             for b in reversed(range(blocks)):
                 rows = pl.ds(b * BLOCK, BLOCK)
-                (leave,) = columns(b, h, LEAVE)
                 state = carry.astype(BF16)
-                kgrad_ref[rows, lanes] = (
-                    attn[h, rows, :] + leave * mm(vb[h, rows, :], state, NT)
-                ).astype(BF16)
+                kgrad_ref[rows, lanes] = (attn[h, rows, :] + mm(vkeyed[h, rows, :], state, NT)).astype(BF16)
                 vgrad_ref[rows, lanes] = (gbuf[h, rows, :] + mm(keyed[h, rows, :], state)).astype(BF16)
                 if b:
                     carry = blocal[b, h] + passrow[b, pl.ds(h, 1), :] * carry
@@ -448,6 +467,12 @@
     for g in range(groups):
         wait_all(g, *b2)
         lax.fori_loop(g * team, (g + 1) * team, final_part(g), 0, unroll=4)
+
+    lax.fori_loop(1, n_seq, pass_sent, 0)
+    lax.fori_loop(1, n_head, head_sent, 0)
+    for g in range(groups):
+        for route in (f1, f2, b1, b2):
+            sent_all(g, *route)
 
 
 def deliver(*refs):

time: 57.8 us -> 56.1 us (0.971); the launches traced: 57.1 us -> 56 us
  Pallas kernels: 56.5 us -> 55.4 us
    pallas_call x1, Pallas kernels: 52.5 us -> 51.4 us  [body(): pl.pallas_call(functools.partial(kernel, n_seq, n_head, heads, blocks, GR...]
where the time goes in v3:
time: 56.1 us; the launch traced here: 56 us
  Pallas kernels  55.4 us (99%)
  between operations  0.64 us (1%)
    pallas_call x1, Pallas kernels, body(): pl.pallas_call(functools.partial(kernel, n_seq, n_head, heads, blocks, GR...  51.4 us
    pallas_call x1, Pallas kernels, body(): pl.pallas_call(deliver, name='deliver', out_shape=[jax.ShapeDtypeStruct((...  4.01 us

profile of v3, /device:TPU:0, one launch (start us, length us, event | category | flops | bytes accessed | tf_op | source)
XLA Modules:
  0.0 56.0 jit_solution(18091757557465944712)
XLA Ops:
  0.6 51.4 %lightning.1 = (bf16[1024,1024]{1,0:T(8,128)(2,1)S(1)}, bf16[1024,1024]{1,0:T(8,128)(2,1)S(1)}, bf16[1024,1024]{1,0:T(8,128)(2,1)S(1)}, bf16[1024,1024]{1,0:T(8,128)(2,1)S(1)}, bf16[1024,1024]{1,0:T(8,128)(2,1)S(1)}) custom-call(bf16[1024,1024]{1,0:T(8,128)(2,1)} %q_hbm.1, bf16[1024,1024]{1,0:T(8,128)(2,1)} %k_hbm.1, bf16[1024,1024]{1,0:T(8,128)(2,1)} %v_hbm.1, ...), custom_call_target="tpu_custom_call" | custom-call | tf_op jit(solution)/shard_map/lightning/pallas_call | solution.py:503
  52.0 4.0 %deliver.1 = (bf16[1024,1024]{1,0:T(8,128)(2,1)}, bf16[1024,1024]{1,0:T(8,128)(2,1)}, bf16[1024,1024]{1,0:T(8,128)(2,1)}, bf16[1024,1024]{1,0:T(8,128)(2,1)}, bf16[1024,1024]{1,0:T(8,128)(2,1)}) custom-call(bf16[1024,1024]{1,0:T(8,128)(2,1)S(1)} %get-tuple-element.10.refs_0_, bf16[1024,1024]{1,0:T(8,128)(2,1)S(1)} %get-tuple-element.11.refs_1_, ...), custom_call_target="tpu_custom_call" | custom-call | tf_op jit(solution)/shard_map/deliver/pallas_call | solution.py:542

commit v4 on v3

--- a/solution.py
+++ b/solution.py
@@ -16,6 +16,7 @@
 SPLIT_F = (4, 4)
 SPLIT_B = (4, 4)
 UNROLL = True
+TEAM = 2
 MESH = pl.DeviceIdType.MESH
 F32 = jnp.float32
 BF16 = jnp.bfloat16
@@ -51,9 +52,9 @@
 def kernel(
     n_seq, n_head, heads, blocks, groups,
     q_hbm, k_hbm, v_hbm, gate_hbm, og_hbm, decay_hbm, doc_hbm, gain_hbm,
-    gated_ref, ggrad_ref, qgrad_ref, kgrad_ref, vgrad_ref,
+    gated_ref, ggrad_ref, qgrad_ref, attn, gbuf, keyed, qkeyed, bheld,
     qb, kb, vb, gateb, ogb, in_sem, decay_ref, doc_ref, gain_ref, small_sem,
-    crow, passrow, cols, mask, wbuf, pbuf, attn, gbuf, keyed, qkeyed, agrad,
+    crow, leave_rows, passrow, cols, mask, wbuf, pbuf, agrad,
     local, blocal, held, acc, norm,
     passall, fsend, frecv, fcarry, fin, bsend, brecv, bcarry, bin_, sums,
     ps, pr, f1s, f1r, f2s, f2r, b1s, b1r, b2s, b2r, hs, hr,
@@ -124,6 +125,7 @@
         passing = jnp.where(r_last == 0.0, jnp.exp(c_last), 0.0)
         passing = jnp.broadcast_to(passing, (heads, HD))
         crow[b] = c
+        leave_rows[b] = leave
         passrow[b] = passing
         total = passing if total is None else total * passing
         hi, mid, low = pieces(jnp.concatenate([c, enter, leave, r], axis=0))
@@ -221,10 +223,8 @@
             state = None
             for b in range(blocks):
                 rows = pl.ds(b * BLOCK, BLOCK)
-                (leave,) = columns(b, h, LEAVE)
-                key = (kb[h, rows, :].astype(F32) * leave).astype(BF16)
-                keyed[h, rows, :] = key
-                part = mm(key, vb[h, rows, :], TN)
+                key_t = kb[h, rows, :].T.astype(F32) * leave_rows[b, pl.ds(h, 1), :]
+                part = mm(key_t.astype(BF16), vb[h, rows, :])
                 local[b, h] = part
                 state = part if state is None else passrow[b, pl.ds(h, 1), :] * state + part
             put_bands(fsend, g, h, state)
@@ -233,7 +233,7 @@
         return go
 
     for g in range(groups):
-        lax.fori_loop(g * team, (g + 1) * team, local_states(g), 0)
+        lax.fori_loop(g * team, (g + 1) * team, local_states(g), 0, unroll=4)
         start_all(g, *f1)
 
     for b in range(blocks):
@@ -247,6 +247,7 @@
             mask[b, :, i * HD : (i + 1) * HD] = jnp.where(same & (j <= t), jnp.inf, -jnp.inf)
 
     tiles = [(0, 0), (1, 0), (1, 1)]
+    qkeyed_t = keyed
 
     def inside_part(h, _):
         load(2, h).wait()
@@ -254,7 +255,11 @@
             rows = pl.ds(b * BLOCK, BLOCK)
             cum, enter = columns(b, h, CUM, ENTER)
             query = qb[h, rows, :]
-            qkeyed[h, rows, :] = (query.astype(F32) * enter).astype(BF16)
+            scaled = (query.astype(F32) * enter).astype(BF16)
+            qkeyed[h, rows, :] = scaled
+            turned = scaled.T
+            for i in range(BLOCK // HD):
+                qkeyed_t[h, pl.ds(b * BLOCK + i * HD, HD), :] = turned[:, i * HD : (i + 1) * HD]
             row = crow[b, pl.ds(h, 1), :]
             out = [None, None]
             for index, (ti, tj) in enumerate(tiles):
@@ -378,7 +383,8 @@
                 rows = pl.ds(b * BLOCK, BLOCK)
                 ag = (norm[0, rows, :] * gbuf[h, rows, :] - attn[h, rows, :] * norm[1, rows, :]).astype(BF16)
                 agrad[h, rows, :] = ag
-                part = mm(qkeyed[h, rows, :], ag, TN)
+                turned = [qkeyed_t[h, pl.ds(b * BLOCK + i * HD, HD), :] for i in range(BLOCK // HD)]
+                part = mm(jnp.concatenate(turned, axis=1), ag)
                 blocal[b, h] = part
                 state = part if state is None else part + passrow[b, pl.ds(h, 1), :] * state
             put_bands(bsend, g, h, state)
@@ -405,6 +411,7 @@
             query = qb[h, rows, :]
             key = kb[h, rows, :]
             value = vb[h, rows, :]
+            keyed[h, rows, :] = (key.astype(F32) * leave).astype(BF16)
             vkeyed[h, rows, :] = (value.astype(F32) * leave).astype(BF16)
             ag = agrad[h, rows, :]
             query_t, ag_t = query.T, ag.T
@@ -449,15 +456,17 @@
 
     lax.fori_loop(SPLIT_B[-1], heads, back_part, 0)
 
-    def final_part(g):
+    lax.fori_loop(1, n_seq, pass_sent, 0)
+    lax.fori_loop(1, n_head, head_sent, 0)
+    for g in range(groups):
+        for route in (f1, f2, b1):
+            sent_all(g, *route)
+
+    def back_states(g):
         def go(h, _):
-            lanes = pl.ds(pl.multiple_of(h * HD, HD), HD)
             carry = get_bands(bin_, g, h)
             for b in reversed(range(blocks)):
-                rows = pl.ds(b * BLOCK, BLOCK)
-                state = carry.astype(BF16)
-                kgrad_ref[rows, lanes] = (attn[h, rows, :] + mm(vkeyed[h, rows, :], state, NT)).astype(BF16)
-                vgrad_ref[rows, lanes] = (gbuf[h, rows, :] + mm(keyed[h, rows, :], state)).astype(BF16)
+                bheld[b, h] = carry.astype(BF16)
                 if b:
                     carry = blocal[b, h] + passrow[b, pl.ds(h, 1), :] * carry
             return 0
@@ -466,23 +475,54 @@
 
     for g in range(groups):
         wait_all(g, *b2)
-        lax.fori_loop(g * team, (g + 1) * team, final_part(g), 0, unroll=4)
-
-    lax.fori_loop(1, n_seq, pass_sent, 0)
-    lax.fori_loop(1, n_head, head_sent, 0)
-    for g in range(groups):
-        for route in (f1, f2, b1, b2):
-            sent_all(g, *route)
-
-
-def deliver(*refs):
-    count = len(refs) // 2
-    sems = refs[-1]
-    copies = [pltpu.make_async_copy(refs[i], refs[count + i], sems.at[i]) for i in range(count)]
-    for copy in copies:
+        lax.fori_loop(g * team, (g + 1) * team, back_states(g), 0, unroll=True)
+    for g in range(groups):
+        sent_all(g, *b2)
+
+
+def finish(
+    heads, blocks,
+    gated_ref, ggrad_ref, qgrad_ref, kpart, vpart, keyed, vkeyed, bheld,
+    gated_hbm, ggrad_hbm, qgrad_hbm, kgrad_hbm, vgrad_hbm,
+    kout, vout, sems,
+):
+    first = [
+        pltpu.make_async_copy(src, dst, sems.at[i, 0])
+        for i, (src, dst) in enumerate(
+            ((gated_ref, gated_hbm), (ggrad_ref, ggrad_hbm), (qgrad_ref, qgrad_hbm))
+        )
+    ]
+    for copy in first:
         copy.start()
-    for copy in copies:
+
+    def strip(i, p):
+        src, dst = ((kout, kgrad_hbm), (vout, vgrad_hbm))[i]
+        lanes = pl.ds(pl.multiple_of(p * TEAM * HD, HD), TEAM * HD)
+        return pltpu.make_async_copy(src.at[:, lanes], dst.at[:, lanes], sems.at[3 + i, p])
+
+    def go(p, _):
+        for i in range(TEAM):
+            h = p * TEAM + i
+            lanes = pl.ds(pl.multiple_of(h * HD, HD), HD)
+            for b in range(blocks):
+                rows = pl.ds(b * BLOCK, BLOCK)
+                state = bheld[b, h]
+                kout[rows, lanes] = (kpart[h, rows, :] + mm(vkeyed[h, rows, :], state, NT)).astype(BF16)
+                vout[rows, lanes] = (vpart[h, rows, :] + mm(keyed[h, rows, :], state)).astype(BF16)
+        strip(0, p).start()
+        strip(1, p).start()
+        return 0
+
+    lax.fori_loop(0, heads // TEAM, go, 0)
+    for copy in first:
         copy.wait()
+
+    def done(p, _):
+        strip(0, p).wait()
+        strip(1, p).wait()
+        return 0
+
+    lax.fori_loop(0, heads // TEAM, done, 0)
 
 
 def solution(mesh):
@@ -503,9 +543,10 @@
         outs = pl.pallas_call(
             functools.partial(kernel, n_seq, n_head, heads, blocks, GROUPS),
             name="lightning",
-            out_shape=[pltpu.VMEM((rows, width), BF16)] * 5,
+            out_shape=[pltpu.VMEM((rows, width), BF16)] * 3
+            + [big(F32), big(F32), big(BF16), big(BF16), pltpu.VMEM((blocks, heads, HD, HD), BF16)],
             in_specs=[hbm] * 8,
-            out_specs=[whole] * 5,
+            out_specs=[whole] * 8,
             scratch_shapes=[
                 big(BF16), big(BF16), big(BF16), big(BF16), big(BF16), dma((5, heads)),
                 pltpu.VMEM((heads, rows), F32),
@@ -513,12 +554,13 @@
                 pltpu.VMEM((8, HD), F32),
                 dma((3,)),
                 pltpu.VMEM((blocks, heads, BLOCK), F32),
+                pltpu.VMEM((blocks, heads, BLOCK), F32),
                 pltpu.VMEM((blocks, heads, HD), F32),
                 pltpu.VMEM((blocks, BLOCK, HD), BF16),
                 pltpu.VMEM((blocks, BLOCK, BLOCK), F32),
                 pltpu.VMEM((heads, blocks, 3, HALF, HALF), BF16),
                 pltpu.VMEM((heads, blocks, 3, HALF, HALF), BF16),
-                big(F32), big(F32), big(BF16), big(BF16), big(BF16),
+                big(BF16),
                 pltpu.VMEM((blocks, heads, HD, HD), F32),
                 pltpu.VMEM((blocks, heads, HD, HD), F32),
                 pltpu.VMEM((blocks, heads, HD, HD), BF16),
@@ -532,7 +574,7 @@
                 dma((n_head,)), dma((n_head,)),
             ],
             compiler_params=pltpu.CompilerParams(
-                collective_id=0, has_side_effects=True, vmem_limit_bytes=50 << 20
+                collective_id=0, has_side_effects=True, vmem_limit_bytes=38 << 20
             ),
         )(
             queries, key_rows, value_rows, gate_input, out_grad, log_decay,
@@ -540,13 +582,17 @@
         )
         return tuple(
             pl.pallas_call(
-                deliver,
-                name="deliver",
+                functools.partial(finish, heads, blocks),
+                name="finish",
                 out_shape=[jax.ShapeDtypeStruct((rows, width), BF16)] * 5,
-                in_specs=[whole] * 5,
+                in_specs=[whole] * 8,
                 out_specs=[hbm] * 5,
-                scratch_shapes=[dma((5,))],
-                compiler_params=pltpu.CompilerParams(vmem_limit_bytes=1 << 20),
+                scratch_shapes=[
+                    pltpu.VMEM((rows, width), BF16),
+                    pltpu.VMEM((rows, width), BF16),
+                    dma((5, heads // TEAM)),
+                ],
+                compiler_params=pltpu.CompilerParams(vmem_limit_bytes=6 << 20),
             )(*[pltpu.with_memory_space_constraint(out, pltpu.VMEM) for out in outs])
         )
 

time: 56.1 us -> 53.9 us (0.961)
  Pallas kernels: 55.4 us -> 53.2 us
    pallas_call x1, Pallas kernels: 51.4 us -> 49.1 us  [body(): pl.pallas_call(functools.partial(kernel, n_seq, n_head, heads, blocks, GR...]
where the time goes in v4:
time: 53.9 us; the launch traced here: 53.8 us
  Pallas kernels  53.2 us (99%)
  between operations  0.64 us (1%)
    pallas_call x1, Pallas kernels, body(): pl.pallas_call(functools.partial(kernel, n_seq, n_head, heads, blocks, GR...  49.1 us
    pallas_call x1, Pallas kernels, body(): pl.pallas_call(functools.partial(finish, heads, blocks), name='finish', o...  4.09 us

profile of v4, /device:TPU:0, one launch (start us, length us, event | category | flops | bytes accessed | tf_op | source)
XLA Modules:
  0.0 53.8 jit_solution(4391381118923597324)
XLA Ops:
  0.6 49.1 %lightning.1 = (bf16[1024,1024]{1,0:T(8,128)(2,1)S(1)}, bf16[1024,1024]{1,0:T(8,128)(2,1)S(1)}, bf16[1024,1024]{1,0:T(8,128)(2,1)S(1)}, f32[8,1024,128]{2,1,0:T(...) custom-call(bf16[1024,1024]{1,0:T(8,128)(2,1)} %q_hbm.1, ...), custom_call_target="tpu_custom_call" | custom-call | tf_op jit(solution)/shard_map/lightning/pallas_call | solution.py:543
  49.7 4.1 %finish.1 = (bf16[1024,1024]{1,0:T(8,128)(2,1)}, bf16[1024,1024]{1,0:T(8,128)(2,1)}, bf16[1024,1024]{1,0:T(8,128)(2,1)}, bf16[1024,1024]{1,0:T(8,128)(2,1)}, bf16[1024,1024]{1,0:T(8,128)(2,1)}) custom-call(bf16[1024,1024]{1,0:T(8,128)(2,1)S(1)} %get-tuple-element.13.gated_ref, bf16[1024,1024]{1,0:T(8,128)(2,1)S(1)} %get-tuple-element.14.ggrad_ref, ...), custom_call_target="tpu_custom_call" | custom-call | tf_op jit(solution)/shard_map/finish/pallas_call | solution.py:584

commit v5 on v4

--- a/solution.py
+++ b/solution.py
@@ -56,8 +56,8 @@
     qb, kb, vb, gateb, ogb, in_sem, decay_ref, doc_ref, gain_ref, small_sem,
     crow, leave_rows, passrow, cols, mask, wbuf, pbuf, agrad,
     local, blocal, held, acc, norm,
-    passall, fsend, frecv, fcarry, fin, bsend, brecv, bcarry, bin_, sums,
-    ps, pr, f1s, f1r, f2s, f2r, b1s, b1r, b2s, b2r, hs, hr,
+    fsend, frecv, fcarry, fin, bsend, brecv, bcarry, bin_, sums,
+    f1s, f1r, f2s, f2r, b1s, b1r, b2s, b2r, hs, hr,
 ):
     seq = lax.axis_index("seq")
     hx = lax.axis_index("head")
@@ -104,9 +104,6 @@
     lax.fori_loop(0, heads, start_kv, 0)
     lax.fori_loop(1, n_seq, greet_seq, 0)
     lax.fori_loop(1, n_head, greet_head, 0)
-    lax.fori_loop(0, heads, start_rest(2), 0)
-    lax.fori_loop(0, heads, start_rest(3), 0)
-    lax.fori_loop(0, heads, start_rest(4), 0)
     for copy in small:
         copy.wait()
 
@@ -131,30 +128,9 @@
         hi, mid, low = pieces(jnp.concatenate([c, enter, leave, r], axis=0))
         stacked = jnp.concatenate([hi, mid, low, jnp.zeros_like(hi)], axis=0)
         cols[b] = stacked.T.astype(BF16)
-    passall[seq] = total
-
-    pl.semaphore_wait(barrier, n_seq - 1 + n_head - 1)
-
-    def pass_copy(o):
-        peer = lax.rem(seq + o, n_seq)
-        return pltpu.make_async_remote_copy(
-            src_ref=passall.at[seq], dst_ref=passall.at[seq], send_sem=ps.at[o], recv_sem=pr.at[o],
-            device_id={"seq": peer}, device_id_type=MESH,
-        )
-
-    def pass_start(o, _):
-        pass_copy(o).start()
-        return 0
-
-    def pass_wait(o, _):
-        pass_copy(o).wait_recv()
-        return 0
-
-    def pass_sent(o, _):
-        pass_copy(o).wait_send()
-        return 0
-
-    lax.fori_loop(1, n_seq, pass_start, 0)
+    tail = team * band
+    fsend[0, :, tail : tail + 8, :] = jnp.broadcast_to(total[None], (n_seq, heads, HD))
+    lax.fori_loop(0, heads, start_rest(2), 0)
 
     def pick(h, *quantities):
         row = lax.broadcasted_iota(jnp.int32, (HD, HD), 0)
@@ -171,8 +147,9 @@
 
     def exchange(g, src, dst, s_sem, r_sem, o):
         peer = lax.rem(seq + o, n_seq)
+        part = pl.ds(0, tail + 8 if src is fsend and g == 0 else tail)
         return pltpu.make_async_remote_copy(
-            src_ref=src.at[g, peer], dst_ref=dst.at[g, seq], send_sem=s_sem.at[g, o], recv_sem=r_sem.at[g, o],
+            src_ref=src.at[g, peer, part], dst_ref=dst.at[g, seq, part], send_sem=s_sem.at[g, o], recv_sem=r_sem.at[g, o],
             device_id={"seq": peer}, device_id_type=MESH,
         )
 
@@ -207,7 +184,7 @@
 
     def pass_bands(d, g):
         return jnp.concatenate(
-            [jnp.broadcast_to(passall[d, g * team + i : g * team + i + 1, :], (band, HD)) for i in range(team)],
+            [jnp.broadcast_to(frecv[0, d, tail + g * team + i : tail + g * team + i + 1, :], (band, HD)) for i in range(team)],
             axis=0,
         )
 
@@ -234,7 +211,11 @@
 
     for g in range(groups):
         lax.fori_loop(g * team, (g + 1) * team, local_states(g), 0, unroll=4)
+        if g == 0:
+            pl.semaphore_wait(barrier, n_seq - 1 + n_head - 1)
         start_all(g, *f1)
+    lax.fori_loop(0, heads, start_rest(3), 0)
+    lax.fori_loop(0, heads, start_rest(4), 0)
 
     for b in range(blocks):
         (r_col,) = columns(b, 0, COUNT)
@@ -279,16 +260,16 @@
         return 0
 
     lax.fori_loop(0, SPLIT_F[0], inside_part, 0)
-    lax.fori_loop(1, n_seq, pass_wait, 0)
     for g in range(groups):
         if g:
             lax.fori_loop(SPLIT_F[g - 1], SPLIT_F[g], inside_part, 0)
         wait_all(g, *f1)
-        frecv[g, seq] = fsend[g, seq]
+        mine = pl.ds(0, tail + 8 if g == 0 else tail)
+        frecv[g, seq, mine] = fsend[g, seq, mine]
         fcarry[g, 0] = jnp.zeros((team * band, HD), F32)
 
         def advance(d, carry):
-            carry = pass_bands(d, g) * carry + frecv[g, d]
+            carry = pass_bands(d, g) * carry + frecv[g, d, 0:tail]
             fcarry[g, d + 1] = carry
             return carry
 
@@ -456,7 +437,6 @@
 
     lax.fori_loop(SPLIT_B[-1], heads, back_part, 0)
 
-    lax.fori_loop(1, n_seq, pass_sent, 0)
     lax.fori_loop(1, n_head, head_sent, 0)
     for g in range(groups):
         for route in (f1, f2, b1):
@@ -539,6 +519,7 @@
         dma = pltpu.SemaphoreType.DMA
         big = lambda kind: pltpu.VMEM((heads, rows, HD), kind)
         states = pltpu.VMEM((GROUPS, n_seq, team * band, HD), F32)
+        wide = pltpu.VMEM((GROUPS, n_seq, team * band + 8, HD), F32)
         seq_sems = dma((GROUPS, n_seq))
         outs = pl.pallas_call(
             functools.partial(kernel, n_seq, n_head, heads, blocks, GROUPS),
@@ -566,10 +547,8 @@
                 pltpu.VMEM((blocks, heads, HD, HD), BF16),
                 pltpu.VMEM((2, rows, HD), F32),
                 pltpu.VMEM((2, rows, HD), F32),
-                pltpu.VMEM((n_seq, heads, HD), F32),
-                states, states, states, states, states, states, states, states,
+                wide, wide, states, states, states, states, states, states,
                 pltpu.VMEM((n_head, 16, HD), F32),
-                dma((n_seq,)), dma((n_seq,)),
                 seq_sems, seq_sems, seq_sems, seq_sems, seq_sems, seq_sems, seq_sems, seq_sems,
                 dma((n_head,)), dma((n_head,)),
             ],

time: 53.9 us -> 53 us (0.983)
  Pallas kernels: 53.2 us -> 52.2 us
    pallas_call x1, Pallas kernels: 49.1 us -> 48.1 us  [body(): pl.pallas_call(functools.partial(kernel, n_seq, n_head, heads, blocks, GR...]
where the time goes in v5:
time: 53 us; the launch traced here: 52.8 us
  Pallas kernels  52.2 us (98%)
  between operations  0.64 us (1%)
    pallas_call x1, Pallas kernels, body(): pl.pallas_call(functools.partial(kernel, n_seq, n_head, heads, blocks, GR...  48.1 us
    pallas_call x1, Pallas kernels, body(): pl.pallas_call(functools.partial(finish, heads, blocks), name='finish', o...  4.09 us

profile of v5, /device:TPU:0, one launch (start us, length us, event | category | flops | bytes accessed | tf_op | source)
XLA Modules:
  0.0 52.8 jit_solution(16136688469278779677)
XLA Ops:
  0.6 48.1 %lightning.1 = (bf16[1024,1024]{1,0:T(8,128)(2,1)S(1)}, bf16[1024,1024]{1,0:T(8,128)(2,1)S(1)}, bf16[1024,1024]{1,0:T(8,128)(2,1)S(1)}, f32[8,1024,128]{2,1,0:T(...) custom-call(bf16[1024,1024]{1,0:T(8,128)(2,1)} %q_hbm.1, ...), custom_call_target="tpu_custom_call" | custom-call | tf_op jit(solution)/shard_map/lightning/pallas_call | solution.py:524
  48.8 4.1 %finish.1 = (bf16[1024,1024]{1,0:T(8,128)(2,1)}, bf16[1024,1024]{1,0:T(8,128)(2,1)}, bf16[1024,1024]{1,0:T(8,128)(2,1)}, bf16[1024,1024]{1,0:T(8,128)(2,1)}, bf16[1024,1024]{1,0:T(8,128)(2,1)}) custom-call(bf16[1024,1024]{1,0:T(8,128)(2,1)S(1)} %get-tuple-element.13.gated_ref, bf16[1024,1024]{1,0:T(8,128)(2,1)S(1)} %get-tuple-element.14.ggrad_ref, ...), custom_call_target="tpu_custom_call" | custom-call | tf_op jit(solution)/shard_map/finish/pallas_call | solution.py:563

commit v6 on v5

--- a/solution.py
+++ b/solution.py
@@ -14,7 +14,7 @@
 EPSILON = 1e-06
 GROUPS = 2
 SPLIT_F = (4, 4)
-SPLIT_B = (4, 4)
+SPLIT_B = (3, 4)
 UNROLL = True
 TEAM = 2
 MESH = pl.DeviceIdType.MESH
@@ -146,7 +146,7 @@
         return [both[:, i * HD : (i + 1) * HD] for i in range(len(quantities))]
 
     def exchange(g, src, dst, s_sem, r_sem, o):
-        peer = lax.rem(seq + o, n_seq)
+        peer = lax.rem(seq + 5 * o, n_seq)
         part = pl.ds(0, tail + 8 if src is fsend and g == 0 else tail)
         return pltpu.make_async_remote_copy(
             src_ref=src.at[g, peer, part], dst_ref=dst.at[g, seq, part], send_sem=s_sem.at[g, o], recv_sem=r_sem.at[g, o],
@@ -273,7 +273,7 @@
             fcarry[g, d + 1] = carry
             return carry
 
-        lax.fori_loop(0, n_seq - 1, advance, jnp.zeros((team * band, HD), F32))
+        lax.fori_loop(0, n_seq - 1, advance, jnp.zeros((team * band, HD), F32), unroll=UNROLL)
         start_all(g, *f2)
         fin[g, seq] = fcarry[g, seq]
 
@@ -431,7 +431,7 @@
             bcarry[g, d - 1] = carry
             return carry
 
-        lax.fori_loop(0, n_seq - 1, retreat, jnp.zeros((team * band, HD), F32))
+        lax.fori_loop(0, n_seq - 1, retreat, jnp.zeros((team * band, HD), F32), unroll=UNROLL)
         start_all(g, *b2)
         bin_[g, seq] = bcarry[g, seq]
 

time: 53 us -> 54.2 us (1.023)
  Pallas kernels: 52.2 us -> 53.5 us
    pallas_call x1, Pallas kernels: 48.1 us -> 49.4 us  [body(): pl.pallas_call(functools.partial(kernel, n_seq, n_head, heads, blocks, GR...]
where the time goes in v6:
time: 54.2 us; the launch traced here: 54.1 us
  Pallas kernels  53.5 us (99%)
  between operations  0.64 us (1%)
    pallas_call x1, Pallas kernels, body(): pl.pallas_call(functools.partial(kernel, n_seq, n_head, heads, blocks, GR...  49.4 us
    pallas_call x1, Pallas kernels, body(): pl.pallas_call(functools.partial(finish, heads, blocks), name='finish', o...  4.09 us

profile of v6, /device:TPU:0, one launch (start us, length us, event | category | flops | bytes accessed | tf_op | source)
XLA Modules:
  0.0 54.1 jit_solution(5889788073762087704)
XLA Ops:
  0.6 49.4 %lightning.1 = (bf16[1024,1024]{1,0:T(8,128)(2,1)S(1)}, bf16[1024,1024]{1,0:T(8,128)(2,1)S(1)}, bf16[1024,1024]{1,0:T(8,128)(2,1)S(1)}, f32[8,1024,128]{2,1,0:T(...) custom-call(bf16[1024,1024]{1,0:T(8,128)(2,1)} %q_hbm.1, ...), custom_call_target="tpu_custom_call" | custom-call | tf_op jit(solution)/shard_map/lightning/pallas_call | solution.py:524
  50.0 4.1 %finish.1 = (bf16[1024,1024]{1,0:T(8,128)(2,1)}, bf16[1024,1024]{1,0:T(8,128)(2,1)}, bf16[1024,1024]{1,0:T(8,128)(2,1)}, bf16[1024,1024]{1,0:T(8,128)(2,1)}, bf16[1024,1024]{1,0:T(8,128)(2,1)}) custom-call(bf16[1024,1024]{1,0:T(8,128)(2,1)S(1)} %get-tuple-element.13.gated_ref, bf16[1024,1024]{1,0:T(8,128)(2,1)S(1)} %get-tuple-element.14.ggrad_ref, ...), custom_call_target="tpu_custom_call" | custom-call | tf_op jit(solution)/shard_map/finish/pallas_call | solution.py:563
